TPU v7x, 512 devices: a whole 4x4x16 slice. The times are simulated.
512 devices in a mesh: ctx: 64 (over y, z), ch: 8 (over x, core).
Axes of the slice: x: 4, y: 4, z: 16, core: 2. Of those that a mesh axis runs over, the one named last changes fastest.
Arguments:
- q_stream: bfloat16 [16384, 2048], P('ctx', 'ch'), may hold values from -6 to 6
- k_stream: bfloat16 [16384, 2048], P('ctx', 'ch'), may hold values from -6 to 6
- v_stream: bfloat16 [16384, 2048], P('ctx', 'ch'), may hold values from -6 to 6
- short_taps: float32 [3, 3, 2048], P(None, None, 'ch'), may hold values from -3 to 3
- short_bias: float32 [3, 2048], P(None, 'ch'), may hold values from -3 to 3
- long_filter: float32 [16384, 2048], P('ctx', 'ch'), may hold values from -0.046875 to 0.046875
- skip_gain: float32 [2048], P('ch'), may hold values from -4 to 4
- out_weight: bfloat16 [2048, 2048], P('ch'), may hold values from -0.1875 to 0.1875
- out_bias: float32 [2048], P('ch'), may hold values from -3 to 3
Outputs:
- mixed: bfloat16 [2048, 16384], P('ch', 'ctx')
All inputs are finite; a program needn't handle non-finite values.
Results may differ from a plain program's by a relative error of at most 0.0049.
Values may be sent and summed in bfloat16 or wider, within the bound.
A program may use at most 64 MiB of HBM per device.

v0:
```python
import math

import jax
import jax.numpy as jnp
from jax import lax
from jax.sharding import PartitionSpec as P

EXACT = lax.Precision.HIGHEST


def from_behind(shard, axis, by):
    length = lax.axis_size(axis)
    pairs = [(i, i + by) for i in range(length) if 0 <= i + by < length]
    return lax.ppermute(shard, axis, pairs)


def angles(left_idx, right_idx, length):
    product = left_idx[:, None] * right_idx[None, :] % length
    phase = product.astype(jnp.float32) * (2.0 * math.pi / length)
    return (jnp.cos(phase), jnp.sin(phase))


def contract(pattern, table, values):
    return jnp.einsum(pattern, table, values, precision=EXACT)


def rotate(pattern, tables, real_part, imag_part, orient):
    cos_table, sin_table = tables
    if imag_part is None:
        return (
            contract(pattern, cos_table, real_part),
            orient * contract(pattern, sin_table, real_part),
        )
    real_out = contract(pattern, cos_table, real_part) - orient * contract(
        pattern, sin_table, imag_part
    )
    imag_out = contract(pattern, cos_table, imag_part) + orient * contract(
        pattern, sin_table, real_part
    )
    return (real_out, imag_out)


def twiddle(real_part, imag_part, cos_table, sin_table, orient):
    return (
        real_part * cos_table - orient * imag_part * sin_table,
        imag_part * cos_table + orient * real_part * sin_table,
    )


def multiply(first, second):
    return (
        first[0] * second[0] - first[1] * second[1],
        first[0] * second[1] + first[1] * second[0],
    )


def sequence_conv(stacked):
    ctx_count = lax.axis_size("ctx")
    row_pairs = 2 * ctx_count
    tok_rows = stacked.shape[1]
    chan_local = stacked.shape[2]
    col_width = tok_rows // ctx_count
    full_length = row_pairs * tok_rows
    my_index = lax.axis_index("ctx")
    forward_rows = angles(jnp.arange(row_pairs), jnp.arange(ctx_count), row_pairs)
    column_tables = angles(jnp.arange(tok_rows), jnp.arange(tok_rows), tok_rows)
    inverse_rows = angles(jnp.arange(ctx_count), jnp.arange(row_pairs), row_pairs)
    column_index = my_index * col_width + jnp.arange(col_width)
    early_cos, early_sin = angles(jnp.arange(row_pairs), column_index, full_length)
    pair_index = 2 * my_index + jnp.arange(2)
    late_cos, late_sin = angles(pair_index, jnp.arange(tok_rows), full_length)
    real_part, imag_part = rotate(
        "kr,srjc->skjc",
        forward_rows,
        lax.all_to_all(
            stacked.reshape(2, 1, tok_rows, chan_local),
            "ctx",
            split_axis=2,
            concat_axis=1,
            tiled=True,
        ),
        None,
        -1.0,
    )
    spread = twiddle(
        real_part, imag_part, early_cos[None, :, :, None], early_sin[None, :, :, None], -1.0
    )
    parts = (
        lax.all_to_all(spread[0], "ctx", split_axis=1, concat_axis=2, tiled=True),
        lax.all_to_all(spread[1], "ctx", split_axis=1, concat_axis=2, tiled=True),
    )
    spectra = rotate("mj,sajc->samc", column_tables, parts[0], parts[1], -1.0)
    product = multiply((spectra[0][0], spectra[1][0]), (spectra[0][1], spectra[1][1]))
    real_back, imag_back = rotate("mj,amc->ajc", column_tables, product[0], product[1], 1.0)
    joined = twiddle(real_back, imag_back, late_cos[:, :, None], late_sin[:, :, None], 1.0)
    parts = (
        lax.all_to_all(joined[0], "ctx", split_axis=1, concat_axis=0, tiled=True),
        lax.all_to_all(joined[1], "ctx", split_axis=1, concat_axis=0, tiled=True),
    )
    cos_table, sin_table = inverse_rows
    ordered = (
        contract("rk,kjc->rjc", cos_table, parts[0]) - contract("rk,kjc->rjc", sin_table, parts[1])
    ) / full_length
    returned = lax.all_to_all(ordered, "ctx", split_axis=0, concat_axis=1, tiled=True)
    return returned.reshape(tok_rows, chan_local)


def shards(
    q_stream,
    k_stream,
    v_stream,
    short_taps,
    short_bias,
    long_filter,
    skip_gain,
    out_weight,
    out_bias,
):
    tok_rows = q_stream.shape[0]
    tails = jnp.stack([q_stream[-2:], k_stream[-2:], v_stream[-2:]])
    earlier = from_behind(tails, "ctx", 1)
    streams = jnp.stack([q_stream, k_stream, v_stream]).astype(jnp.float32)
    padded = jnp.concatenate([earlier.astype(jnp.float32), streams], axis=1)
    shortened = (
        short_taps[:, 0, None, :] * padded[:, :tok_rows]
        + short_taps[:, 1, None, :] * padded[:, 1 : tok_rows + 1]
        + short_taps[:, 2, None, :] * padded[:, 2:]
        + short_bias[:, None, :]
    )
    gated = shortened[1] * shortened[2]
    stacked = jnp.stack([gated, long_filter])
    convolved = sequence_conv(stacked)
    operator = (shortened[0] * (convolved + skip_gain * gated)).astype(jnp.bfloat16)
    summed = lax.psum_scatter(
        lax.dot_general(
            out_weight, operator, (((0,), (1,)), ((), ())), preferred_element_type=jnp.float32
        ),
        "ch",
        scatter_dimension=0,
        tiled=True,
    )
    return (summed + out_bias[:, None]).astype(jnp.bfloat16)


def solution(mesh):
    return jax.shard_map(
        shards,
        mesh=mesh,
        in_specs=(
            P("ctx", "ch"),
            P("ctx", "ch"),
            P("ctx", "ch"),
            P(None, None, "ch"),
            P(None, "ch"),
            P("ctx", "ch"),
            P("ch"),
            P("ch", None),
            P("ch"),
        ),
        out_specs=P("ch", "ctx"),
        check_vma=False,
    )
```

profile of v0, /device:TPU:1, one launch (start us, length us, event | category | flops | bytes accessed | tf_op | source)
XLA Modules:
  0.0 360.2 jit_solution(1399777371781088860)
XLA Ops:
  8.1 4.4 %collective-permute-start = (bf16[3,2,256]{2,1,0:T(2,128)(2,1)S(1)}, bf16[3,2,256]{2,1,0:T(2,128)(2,1)S(1)}, u32[]{:S(2)}, u32[]{:S(2)}) collective-permute-start(bf16[3,2,256]{2,1,0:T(2,128)(2,1)S(1)} %pad_maximum_fusion.1), channel_id=1, source_target_pairs={{0,8},{8,16},{16,24},{24,32},{32,40},{40,48},{48,56},{56,64},{64,7... | collective-permute-start | bytes 9224 | tf_op jit(solution)/shard_map/ppermute | solution.py:14
  13.3 1.1 maximum_convert_fusion
  16.4 1.2 copy.32
  17.6 18.5 %all-to-all-start = ((f32[2,1,256,256]{3,0,1,2:T(2,128)}), f32[2,1,256,256]{3,0,1,2:T(2,128)S(1)}, u32[]{:S(2)}, u32[]{:S(2)}) async-start(f32[2,1,256,256]{3,0,1,2:T(2,128)} %copy.32), calls=%async_computation | async-start | bytes 1048576 | tf_op jit(solution)/shard_map/all_to_all | solution.py:75
  36.2 27.8 %all-to-all-done = f32[2,1,256,256]{3,0,1,2:T(2,128)S(1)} async-done(((f32[2,1,256,256]{3,0,1,2:T(2,128)}), f32[2,1,256,256]{3,0,1,2:T(2,128)S(1)}, u32[]{:S(2)}, u32[]{:S(2)}) %all-to-all-start) | async-done | bytes 524320 | tf_op jit(solution)/shard_map/all_to_all | solution.py:75
  64.0 1.9 convolution_bitcast_fusion.2
  65.9 2.9 multiply_subtract_fusion
  68.8 2.6 copy.35
  71.5 9.9 %all-to-all-start.1 = ((f32[2,128,4,256]{3,2,0,1:T(4,128)}), f32[2,128,4,256]{3,2,0,1:T(4,128)}, u32[]{:S(2)}, u32[]{:S(2)}) async-start(f32[2,128,4,256]{3,2,0,1:T(4,128)} %copy.35), calls=%async_computation.1 | async-start | bytes 2097152 | tf_op jit(solution)/shard_map/all_to_all | solution.py:89
  81.3 1.4 copy.39
  82.7 47.0 %all-to-all-done.1 = f32[2,128,4,256]{3,2,0,1:T(4,128)} async-done(((f32[2,128,4,256]{3,2,0,1:T(4,128)}), f32[2,128,4,256]{3,2,0,1:T(4,128)}, u32[]{:S(2)}, u32[]{:S(2)}) %all-to-all-start.1) | async-done | bytes 1048608 | tf_op jit(solution)/shard_map/all_to_all | solution.py:89
  129.7 12.1 %all-to-all-start.2 = ((f32[2,128,4,256]{3,2,0,1:T(4,128)}), f32[2,128,4,256]{3,2,0,1:T(4,128)S(1)}, u32[]{:S(2)}, u32[]{:S(2)}) async-start(f32[2,128,4,256]{3,2,0,1:T(4,128)} %copy.39), calls=%async_computation.2 | async-start | bytes 2097152 | tf_op jit(solution)/shard_map/all_to_all | solution.py:90
  141.9 2.8 copy.37
  144.7 1.5 copy.38
  146.2 2.9 fusion.33
  149.1 43.0 %all-to-all-done.2 = f32[2,128,4,256]{3,2,0,1:T(4,128)S(1)} async-done(((f32[2,128,4,256]{3,2,0,1:T(4,128)}), f32[2,128,4,256]{3,2,0,1:T(4,128)S(1)}, u32[]{:S(2)}, u32[]{:S(2)}) %all-to-all-start.2) | async-done | bytes 1048608 | tf_op jit(solution)/shard_map/all_to_all | solution.py:90
  192.1 1.5 copy.41
  193.6 1.5 copy.42
  195.1 2.0 fusion.31
  197.1 2.0 fusion.3
  199.1 2.0 fusion.1
  201.2 1.6 fusion.11
  202.8 1.6 fusion.15
  204.3 1.6 convolution_add_fusion
  205.9 1.8 add_bitcast_fusion
  208.7 9.9 %all-to-all-start.3 = ((f32[2,256,256]{2,0,1:T(2,128)}), f32[2,256,256]{2,0,1:T(2,128)S(1)}, u32[]{:S(2)}, u32[]{:S(2)}) async-start(f32[2,256,256]{2,0,1:T(2,128)} %copy.45), calls=%async_computation.3 | async-start | bytes 1048576 | tf_op jit(solution)/shard_map/all_to_all | solution.py:97
  219.7 28.0 %all-to-all-done.3 = f32[2,256,256]{2,0,1:T(2,128)S(1)} async-done(((f32[2,256,256]{2,0,1:T(2,128)}), f32[2,256,256]{2,0,1:T(2,128)S(1)}, u32[]{:S(2)}, u32[]{:S(2)}) %all-to-all-start.3) | async-done | bytes 524320 | tf_op jit(solution)/shard_map/all_to_all | solution.py:97
  247.7 8.9 %all-to-all-start.4 = ((f32[2,256,256]{2,0,1:T(2,128)}), f32[2,256,256]{2,0,1:T(2,128)S(1)}, u32[]{:S(2)}, u32[]{:S(2)}) async-start(f32[2,256,256]{2,0,1:T(2,128)} %copy.47), calls=%async_computation.4 | async-start | bytes 1048576 | tf_op jit(solution)/shard_map/all_to_all | solution.py:98
  257.8 27.9 %all-to-all-done.4 = f32[2,256,256]{2,0,1:T(2,128)S(1)} async-done(((f32[2,256,256]{2,0,1:T(2,128)}), f32[2,256,256]{2,0,1:T(2,128)S(1)}, u32[]{:S(2)}, u32[]{:S(2)}) %all-to-all-start.4) | async-done | bytes 524320 | tf_op jit(solution)/shard_map/all_to_all | solution.py:98
  287.0 27.4 %all_to_all.93 = f32[64,4,256]{2,1,0:T(4,128)S(1)} all-to-all(f32[64,4,256]{2,1,0:T(4,128)S(1)} %copy.49), channel_id=1, replica_groups=mesh['ctx'=64,'ch'=8] {'ctx'}, dimensions={0} | all-to-all | bytes 524288 | tf_op jit(solution)/shard_map/all_to_all | solution.py:104
  314.5 2.7 convolution_bitcast_fusion
  317.2 34.4 %reduce-scatter.2.cloned.1.call-done = f32[256,256]{0,1:T(8,128)} async-done(((f32[2048,256]{0,1:T(8,128)}), f32[256,256]{0,1:T(8,128)}) %reduce-scatter.2.cloned.1.call-update) | async-done | bytes 262160 | tf_op jit(solution)/shard_map/reduce_scatter | solution.py:134
  (42 shorter events, 10.9 us)
Async XLA Ops:
  6.5 307.9 %copy-start = (bf16[256,2048]{1,0:T(8,128)(2,1)S(1)}, bf16[256,2048]{1,0:T(8,128)(2,1)}, u32[]{:S(2)}) copy-start(bf16[256,2048]{1,0:T(8,128)(2,1)} %param.16) | copy-start | bytes 3145732
  6.5 9.8 %copy-start.3 = (f32[256,256]{1,0:T(8,128)S(1)}, f32[256,256]{1,0:T(8,128)}, u32[]{:S(2)}) copy-start(f32[256,256]{1,0:T(8,128)} %param.14) | copy-start | bytes 786436
  8.1 6.3 %collective-permute-start = (bf16[3,2,256]{2,1,0:T(2,128)(2,1)S(1)}, bf16[3,2,256]{2,1,0:T(2,128)(2,1)S(1)}, u32[]{:S(2)}, u32[]{:S(2)}) collective-permute-start(bf16[3,2,256]{2,1,0:T(2,128)(2,1)S(1)} %pad_maximum_fusion.1), channel_id=1, source_target_pairs={{0,8},{8,16},{16,24},{24,32},{32,40},{40,48},{48,56},{56,64},{64,7... | collective-permute-start | bytes 9224 | tf_op jit(solution)/shard_map/ppermute | solution.py:14
  15.4 0.9 copy-start.2
  17.6 46.4 %all-to-all-start = ((f32[2,1,256,256]{3,0,1,2:T(2,128)}), f32[2,1,256,256]{3,0,1,2:T(2,128)S(1)}, u32[]{:S(2)}, u32[]{:S(2)}) async-start(f32[2,1,256,256]{3,0,1,2:T(2,128)} %copy.32), calls=%async_computation | async-start | bytes 1048576 | tf_op jit(solution)/shard_map/all_to_all | solution.py:75
  71.5 58.3 %all-to-all-start.1 = ((f32[2,128,4,256]{3,2,0,1:T(4,128)}), f32[2,128,4,256]{3,2,0,1:T(4,128)}, u32[]{:S(2)}, u32[]{:S(2)}) async-start(f32[2,128,4,256]{3,2,0,1:T(4,128)} %copy.35), calls=%async_computation.1 | async-start | bytes 2097152 | tf_op jit(solution)/shard_map/all_to_all | solution.py:89
  129.7 62.4 %all-to-all-start.2 = ((f32[2,128,4,256]{3,2,0,1:T(4,128)}), f32[2,128,4,256]{3,2,0,1:T(4,128)S(1)}, u32[]{:S(2)}, u32[]{:S(2)}) async-start(f32[2,128,4,256]{3,2,0,1:T(4,128)} %copy.39), calls=%async_computation.2 | async-start | bytes 2097152 | tf_op jit(solution)/shard_map/all_to_all | solution.py:90
  195.1 2.0 copy-start.1
  208.7 39.0 %all-to-all-start.3 = ((f32[2,256,256]{2,0,1:T(2,128)}), f32[2,256,256]{2,0,1:T(2,128)S(1)}, u32[]{:S(2)}, u32[]{:S(2)}) async-start(f32[2,256,256]{2,0,1:T(2,128)} %copy.45), calls=%async_computation.3 | async-start | bytes 1048576 | tf_op jit(solution)/shard_map/all_to_all | solution.py:97
  247.7 38.0 %all-to-all-start.4 = ((f32[2,256,256]{2,0,1:T(2,128)}), f32[2,256,256]{2,0,1:T(2,128)S(1)}, u32[]{:S(2)}, u32[]{:S(2)}) async-start(f32[2,256,256]{2,0,1:T(2,128)} %copy.47), calls=%async_computation.4 | async-start | bytes 1048576 | tf_op jit(solution)/shard_map/all_to_all | solution.py:98
  256.7 95.0 %reduce-scatter.2.cloned.1.call-start = ((), (), s32[]{:S(2)}) async-start(), calls=%async_computation.7 | async-start | bytes 2359296 | tf_op jit(solution)/shard_map/reduce_scatter | solution.py:134
  285.9 28.6 %copy-start.4 = (f32[256]{0:T(256)S(1)}, f32[256]{0:T(256)}, u32[]{:S(2)}) copy-start(f32[256]{0:T(256)} %param.15) | copy-start | bytes 3076
  314.5 37.2 %copy-start.5 = (f32[256]{0:T(256)S(1)}, f32[256]{0:T(256)}, u32[]{:S(2)}) copy-start(f32[256]{0:T(256)} %param.17) | copy-start | bytes 3076
Sparse Core Ops, SparseCore 0:
  317.4 34.2 reduce-scatter.1
where the time goes:
time: 362 us; the launch traced here: 360 us
  waiting for transfers between devices  208 us (57%)
  starting transfers between devices  63.7 us (18%)
  blocking collectives  27.4 us (8%)
  matrix products  24 us (7%)
  local copies, waits for them, and re-layouts  19.8 us (5%)
  between operations  13.7 us (4%)
    all_to_all x1, waiting for transfers between devices, sequence_conv(): lax.all_to_all(spread[0], 'ctx', split_axis=1, concat_axis=2, tiled=True)  47 us
    all_to_all x1, waiting for transfers between devices, sequence_conv(): lax.all_to_all(spread[1], 'ctx', split_axis=1, concat_axis=2, tiled=True)  43 us
    reduce_scatter x1, waiting for transfers between devices, shards(): lax.psum_scatter(lax.dot_general(out_weight, operator, (((0,), (1,)), (()...  34.4 us
    all_to_all x1, waiting for transfers between devices, sequence_conv(): lax.all_to_all(joined[0], 'ctx', split_axis=1, concat_axis=0, tiled=True)  28 us
    all_to_all x1, waiting for transfers between devices, sequence_conv(): lax.all_to_all(joined[1], 'ctx', split_axis=1, concat_axis=0, tiled=True)  27.9 us
    all_to_all x1, waiting for transfers between devices, sequence_conv(): lax.all_to_all(stacked.reshape(2, 1, tok_rows, chan_local), 'ctx', split_...  27.8 us
    all_to_all x1, blocking collectives, sequence_conv(): lax.all_to_all(ordered, 'ctx', split_axis=0, concat_axis=1, tiled=True)  27.4 us
    dot_general x12, matrix products, contract(): return jnp.einsum(pattern, table, values, precision=EXACT)  21.3 us
  transfers between devices with their start and end apart: 7, of which 6 were waited for; matrix products, arithmetic and copies ran while one was open for 3% of the time, Pallas kernels for 0%

commit v1 on v0

v1 whole, which is shorter than its diff:
```python
import functools

import jax
import jax.numpy as jnp
from jax import lax
from jax.experimental import pallas as pl
from jax.experimental.pallas import tpu as pltpu
from jax.sharding import PartitionSpec as P

MESH = pl.DeviceIdType.MESH
F32 = jnp.float32
BF16 = jnp.bfloat16
LANES = 128
STEP = 16


def remote(src, dst, send_sem, recv_sem, axis, target):
    return pltpu.make_async_remote_copy(
        src_ref=src, dst_ref=dst, send_sem=send_sem, recv_sem=recv_sem,
        device_id={axis: target}, device_id_type=MESH,
    )


def wait_bytes(ref, sem):
    pltpu.make_async_copy(ref, ref, sem).wait()


def kernel(
    ctx_n, ch_n,
    q_ref, k_ref, v_ref, taps_ref, sbias_ref, filt_ref, skip_ref, w_ref, obias_ref,
    out_ref,
    flat, halo_out, halo_in, wide, send_h, send_g, send_y, recv_h, recv_g, recv_y,
    gated_t, query_t, toeplitz, shifted, padded, acc, w_all, w_t, oper,
    send_sem, recv_sem, halo_sem, w_send, w_recv, o_send, o_recv,
):
    me = lax.axis_index("ctx")
    my_ch = lax.axis_index("ch")

    barrier = pltpu.get_barrier_semaphore()

    @pl.loop(1, ctx_n)
    def _(step):
        pl.semaphore_signal(
            barrier, inc=1, device_id={"ctx": lax.rem(me + step, ctx_n)}, device_id_type=MESH)

    @pl.loop(1, ch_n)
    def _(step):
        pl.semaphore_signal(
            barrier, inc=1, device_id={"ch": lax.rem(my_ch + step, ch_n)}, device_id_type=MESH)

    def pack(halves, dst):
        for half in range(2):
            flat[pl.ds(half, 256, stride=2), :] = halves[half]
        dst[...] = flat[...].reshape(ctx_n, 8, LANES).astype(BF16)

    def exchange(src, dst, which):
        @pl.loop(1, ctx_n)
        def _(step):
            target = lax.rem(me + step, ctx_n)
            remote(src.at[target], dst.at[me], send_sem.at[which], recv_sem.at[which],
                   "ctx", target).start()
        dst[me] = src[me]

    pack([filt_ref[pl.ds(half * LANES, LANES), :].T for half in range(2)], send_h)

    tails = [ref[240:256, :].astype(F32)[14:16] for ref in (q_ref, k_ref, v_ref)]
    halo_out[...] = jnp.concatenate(tails + [jnp.zeros((10, 256), F32)], axis=0).astype(BF16)
    for index, ref in enumerate((q_ref, k_ref, v_ref)):
        wide[index, pl.ds(8, 256), :] = ref[...].astype(F32)

    pl.semaphore_wait(barrier, ctx_n + ch_n - 2)

    ahead = lax.rem(me + 1, ctx_n)
    halo_copy = remote(halo_out, halo_in, halo_sem.at[0], halo_sem.at[1], "ctx", ahead)
    halo_copy.start()
    exchange(send_h, recv_h, 0)

    @pl.loop(1, ch_n)
    def _(step):
        target = lax.rem(my_ch + step, ch_n)
        remote(w_ref.at[:, pl.ds(pl.multiple_of(target * 256, 256), 256)], w_all.at[my_ch],
               w_send, w_recv, "ch", target).start()
    w_all[my_ch] = w_ref[:, pl.ds(pl.multiple_of(my_ch * 256, 256), 256)]

    halo_copy.wait()
    before = jnp.where(me > 0, halo_in[...].astype(F32), 0.0)
    for index in range(3):
        wide[index, 6:8, :] = before[2 * index:2 * index + 2, :]

    def short(index, half):
        at = half * LANES
        return (
            taps_ref[index, 0:1, :] * wide[index, pl.ds(6 + at, LANES), :]
            + taps_ref[index, 1:2, :] * wide[index, pl.ds(7 + at, LANES), :]
            + taps_ref[index, 2:3, :] * wide[index, pl.ds(8 + at, LANES), :]
            + sbias_ref[index:index + 1, :]
        )

    for half in range(2):
        gated_t[half] = (short(1, half) * short(2, half)).T
    pack([gated_t[0], gated_t[1]], send_g)
    exchange(send_g, recv_g, 1)

    for half in range(2):
        query_t[half] = short(0, half).T

    wait_bytes(recv_h.at[pl.ds(0, ctx_n - 1)], recv_sem.at[0])
    flat[...] = recv_h[...].astype(F32).reshape(512, LANES)
    keep = (lax.broadcasted_iota(jnp.int32, (LANES, LANES), 1)
            >= lax.broadcasted_iota(jnp.int32, (LANES, LANES), 0))

    @pl.loop(0, 4)
    def _(chan):
        def build(block, earlier):
            for half in range(2):
                row = flat[pl.ds(8 * block + 2 * chan + half, 1), :]
                rolled = pltpu.roll(
                    jnp.broadcast_to(row, (LANES, LANES)), 0, 1, stride=1, stride_axis=0)
                at = pl.multiple_of(256 * block + LANES * half, LANES)
                toeplitz[chan, pl.ds(at, LANES), :] = jnp.where(keep, rolled, earlier).astype(BF16)
                earlier = rolled
            return earlier
        lax.fori_loop(0, ctx_n, build, jnp.zeros((LANES, LANES), F32))

    wait_bytes(recv_g.at[pl.ds(0, ctx_n - 1)], recv_sem.at[1])
    flat[...] = recv_g[...].astype(F32).reshape(512, LANES)
    padded[0:STEP, :] = jnp.zeros((STEP, LANES), F32)

    @pl.loop(0, 4)
    def _(chan):
        for half in range(2):
            padded[pl.ds(STEP + half, 64, stride=2), :] = flat[
                pl.ds(2 * chan + half, 64, stride=8), :]
        for lag in range(STEP):
            shifted[:, pl.ds(lag * LANES, LANES)] = padded[
                pl.ds(STEP - lag, LANES), :].astype(BF16)
        for part in range(8):
            rows = LANES - STEP * part
            product = jnp.dot(
                shifted[0:rows, :], toeplitz[chan, pl.ds(2048 * part, 2048), :],
                preferred_element_type=F32)
            if part == 0:
                acc[...] = product
            else:
                acc[pl.ds(STEP * part, rows), :] += product
        for half in range(2):
            flat[pl.ds(2 * chan + half, 64, stride=8), :] = acc[pl.ds(half, 64, stride=2), :]

    send_y[...] = flat[...].reshape(ctx_n, 8, LANES).astype(BF16)
    exchange(send_y, recv_y, 2)

    wait_bytes(w_all.at[pl.ds(0, ch_n - 1)], w_recv)

    @pl.loop(0, ch_n)
    def _(index):
        w_t[index] = w_all[index].T
    skip_t = jnp.broadcast_to(skip_ref[...], (LANES, 256)).T
    bias_t = jnp.broadcast_to(obias_ref[...], (LANES, 256)).T

    wait_bytes(recv_y.at[pl.ds(0, ctx_n - 1)], recv_sem.at[2])
    flat[...] = recv_y[...].astype(F32).reshape(512, LANES)
    for half in range(2):
        conv = flat[pl.ds(half, 256, stride=2), :]
        oper[my_ch, :, half * LANES:(half + 1) * LANES] = (
            query_t[half] * (conv + skip_t * gated_t[half])).astype(BF16)

    @pl.loop(1, ch_n)
    def _(step):
        target = lax.rem(my_ch + step, ch_n)
        remote(oper.at[my_ch], oper.at[my_ch], o_send, o_recv.at[my_ch], "ch", target).start()

    total = jnp.dot(w_t[my_ch], oper[my_ch], preferred_element_type=F32)
    for step in range(1, ch_n):
        source = lax.rem(my_ch + step, ch_n)
        wait_bytes(oper.at[source], o_recv.at[source])
        total = total + jnp.dot(w_t[source], oper[source], preferred_element_type=F32)
    for half in range(2):
        cut = slice(half * LANES, (half + 1) * LANES)
        out_ref[:, cut] = (total[:, cut] + bias_t).astype(BF16)

    for which, ref in enumerate((send_h, send_g, send_y)):
        wait_bytes(ref.at[pl.ds(0, ctx_n - 1)], send_sem.at[which])
    wait_bytes(w_all.at[pl.ds(0, ch_n - 1)], w_send)
    wait_bytes(oper.at[pl.ds(0, ch_n - 1)], o_send)


def shards(q, k, v, taps, sbias, filt, skip, weight, obias):
    ctx_n, ch_n = lax.axis_size("ctx"), lax.axis_size("ch")
    vmem = pl.BlockSpec(memory_space=pltpu.VMEM)
    message = pltpu.VMEM((ctx_n, 8, LANES), BF16)
    dma = pltpu.SemaphoreType.DMA
    return pl.pallas_call(
        functools.partial(kernel, ctx_n, ch_n),
        out_shape=jax.ShapeDtypeStruct((256, 256), BF16),
        in_specs=[vmem] * 9,
        out_specs=vmem,
        scratch_shapes=[
            pltpu.VMEM((512, LANES), F32),
            pltpu.VMEM((16, 256), BF16),
            pltpu.VMEM((16, 256), BF16),
            pltpu.VMEM((3, 264, 256), F32),
            message, message, message, message, message, message,
            pltpu.VMEM((2, 256, LANES), F32),
            pltpu.VMEM((2, 256, LANES), F32),
            pltpu.VMEM((4, 16384, LANES), BF16),
            pltpu.VMEM((LANES, 2048), BF16),
            pltpu.VMEM((LANES + STEP, LANES), F32),
            pltpu.VMEM((LANES, LANES), F32),
            pltpu.VMEM((ch_n, 256, 256), BF16),
            pltpu.VMEM((ch_n, 256, 256), BF16),
            pltpu.VMEM((ch_n, 256, 256), BF16),
            dma((3,)), dma((3,)), dma((2,)), dma, dma, dma, dma((ch_n,)),
        ],
        compiler_params=pltpu.CompilerParams(
            collective_id=3, has_side_effects=True, vmem_limit_bytes=50 * 2**20),
    )(q, k, v, taps, sbias, filt, skip.reshape(1, -1), weight, obias.reshape(1, -1))


def solution(mesh):
    return jax.shard_map(
        shards,
        mesh=mesh,
        in_specs=(
            P("ctx", "ch"),
            P("ctx", "ch"),
            P("ctx", "ch"),
            P(None, None, "ch"),
            P(None, "ch"),
            P("ctx", "ch"),
            P("ch"),
            P("ch", None),
            P("ch"),
        ),
        out_specs=P("ch", "ctx"),
        check_vma=False,
    )
```

time: 362 us -> 89.8 us (0.25)
  waiting for transfers between devices: 208 us -> 0 us
  Pallas kernels: 0 us -> 81.8 us
  starting transfers between devices: 63.7 us -> 0 us
  blocking collectives: 27.4 us -> 0 us
  matrix products: 24 us -> 0 us
  between operations: 13.7 us -> 0.02 us
  local copies, waits for them, and re-layouts: 19.8 us -> 7.63 us
    all_to_all x5 -> x0, waiting for transfers between devices: 174 us -> none  [the longest x1 47 us: sequence_conv(): lax.all_to_all(spread[0], 'ctx', split_axis=1, concat_axis=2, tiled=True)]
    pallas_call x0 -> x1, Pallas kernels: none -> 81.8 us  [shards(): pl.pallas_call(functools.partial(kernel, ctx_n, ch_n), out_shape=jax.Shap...]
    all_to_all x5 -> x0, starting transfers between devices: 59.3 us -> none  [the longest x1 18.5 us: sequence_conv(): lax.all_to_all(stacked.reshape(2, 1, tok_rows, chan_local), 'ctx', split_...]
    reduce_scatter x1 -> x0, waiting for transfers between devices: 34.4 us -> none  [shards(): lax.psum_scatter(lax.dot_general(out_weight, operator, (((0,), (1,)), (()...]
    all_to_all x1 -> x0, blocking collectives: 27.4 us -> none  [sequence_conv(): lax.all_to_all(ordered, 'ctx', split_axis=0, concat_axis=1, tiled=True)]
    dot_general x13 -> x0, matrix products: 24 us -> none  [the longest x12 21.3 us: contract(): return jnp.einsum(pattern, table, values, precision=EXACT)]
    all_to_all x8 -> x0, local copies, waits for them, and re-layouts: 8.31 us -> none  [the longest x2 4.22 us: sequence_conv(): lax.all_to_all(spread[0], 'ctx', split_axis=1, concat_axis=2, tiled=True)]
    unnamed x14 -> x19, local copies, waits for them, and re-layouts: 0.92 us -> 7.63 us
  transfers between devices with their start and end apart: 7 -> 0, of which waited for: 6 -> 0; matrix products, arithmetic and copies ran while one was open for 3% -> 0% of each run, Pallas kernels for 0% -> 0%
where the time goes in v1:
time: 89.8 us; the launch traced here: 89.5 us
  Pallas kernels  81.8 us (91%)
  local copies, waits for them, and re-layouts  7.63 us (8%)
    pallas_call x1, Pallas kernels, shards(): pl.pallas_call(functools.partial(kernel, ctx_n, ch_n), out_shape=jax.Shap...  81.8 us
    unnamed x19, local copies, waits for them, and re-layouts  7.63 us

profile of v1, /device:TPU:1, one launch (start us, length us, event | category | flops | bytes accessed | tf_op | source)
XLA Modules:
  0.0 89.5 jit_solution(1884734853961968734)
XLA Ops:
  0.0 0.0 copy-start.8
  0.0 0.0 copy-start.7
  0.0 0.7 copy-done.8
  0.7 0.0 copy-done.7
  0.7 0.0 copy-start
  0.7 1.2 %copy-done = bf16[256,2048]{1,0:T(8,128)(2,1)S(1)} copy-done((bf16[256,2048]{1,0:T(8,128)(2,1)S(1)}, bf16[256,2048]{1,0:T(8,128)(2,1)}, u32[]{:S(2)}) %copy-start) | copy-done | bytes 1048600
  1.9 0.0 copy-start.1
  1.9 0.9 %copy-done.1 = f32[256,256]{1,0:T(8,128)S(1)} copy-done((f32[256,256]{1,0:T(8,128)S(1)}, f32[256,256]{1,0:T(8,128)}, u32[]{:S(2)}) %copy-start.1) | copy-done | bytes 262168
  2.9 0.0 copy-start.2
  2.9 0.9 %copy-done.2 = bf16[256,256]{1,0:T(8,128)(2,1)S(1)} copy-done((bf16[256,256]{1,0:T(8,128)(2,1)S(1)}, bf16[256,256]{1,0:T(8,128)(2,1)}, u32[]{:S(2)}) %copy-start.2) | copy-done | bytes 131096
  3.8 0.0 copy-start.3
  3.8 0.9 %copy-done.3 = bf16[256,256]{1,0:T(8,128)(2,1)S(1)} copy-done((bf16[256,256]{1,0:T(8,128)(2,1)S(1)}, bf16[256,256]{1,0:T(8,128)(2,1)}, u32[]{:S(2)}) %copy-start.3) | copy-done | bytes 131096
  4.7 0.0 copy-start.4
  4.7 0.9 %copy-done.4 = bf16[256,256]{1,0:T(8,128)(2,1)S(1)} copy-done((bf16[256,256]{1,0:T(8,128)(2,1)S(1)}, bf16[256,256]{1,0:T(8,128)(2,1)}, u32[]{:S(2)}) %copy-start.4) | copy-done | bytes 131096
  5.6 0.0 copy-start.5
  5.6 0.7 copy-done.5
  6.3 0.0 copy-start.6
  6.3 0.7 copy-done.6
  7.0 81.8 %shard_map.91 = bf16[256,256]{1,0:T(8,128)(2,1)S(1)} custom-call(bf16[256,256]{1,0:T(8,128)(2,1)S(1)} %copy-done.2, bf16[256,256]{1,0:T(8,128)(2,1)S(1)} %copy-done.3, bf16[256,256]{1,0:T(8,128)(2,1)S(1)} %copy-done.4, f32[3,3,256]{2,1,0:T(4,128)S(1)} %copy-done.5, f32[3,256]{1,0:T(4,128)S(1)} %copy-done.6, f32[256,256]{1,0:T(8,128)S(1)} %copy-done.1, ...), custom_call_target="tpu_custom_call" | custom-call | tf_op jit(solution)/shard_map/pallas_call | solution.py:192
  88.8 0.7 copy.11
Async XLA Ops:
  0.0 0.7 copy-start.8
  0.0 0.7 copy-start.7
  0.7 1.2 %copy-start = (bf16[256,2048]{1,0:T(8,128)(2,1)S(1)}, bf16[256,2048]{1,0:T(8,128)(2,1)}, u32[]{:S(2)}) copy-start(bf16[256,2048]{1,0:T(8,128)(2,1)} %w_ref.1) | copy-start | bytes 3145732
  1.9 0.9 %copy-start.1 = (f32[256,256]{1,0:T(8,128)S(1)}, f32[256,256]{1,0:T(8,128)}, u32[]{:S(2)}) copy-start(f32[256,256]{1,0:T(8,128)} %filt_ref.1) | copy-start | bytes 786436
  2.9 0.9 %copy-start.2 = (bf16[256,256]{1,0:T(8,128)(2,1)S(1)}, bf16[256,256]{1,0:T(8,128)(2,1)}, u32[]{:S(2)}) copy-start(bf16[256,256]{1,0:T(8,128)(2,1)} %q_ref.1) | copy-start | bytes 393220
  3.8 0.9 %copy-start.3 = (bf16[256,256]{1,0:T(8,128)(2,1)S(1)}, bf16[256,256]{1,0:T(8,128)(2,1)}, u32[]{:S(2)}) copy-start(bf16[256,256]{1,0:T(8,128)(2,1)} %k_ref.1) | copy-start | bytes 393220
  4.7 0.9 %copy-start.4 = (bf16[256,256]{1,0:T(8,128)(2,1)S(1)}, bf16[256,256]{1,0:T(8,128)(2,1)}, u32[]{:S(2)}) copy-start(bf16[256,256]{1,0:T(8,128)(2,1)} %v_ref.1) | copy-start | bytes 393220
  5.6 0.7 copy-start.5
  6.3 0.7 copy-start.6

commit v2 on v1

v2 whole, which is shorter than its diff:
```python
import functools

import jax
import jax.numpy as jnp
from jax import lax
from jax.experimental import pallas as pl
from jax.experimental.pallas import tpu as pltpu
from jax.sharding import PartitionSpec as P

MESH = pl.DeviceIdType.MESH
F32 = jnp.float32
BF16 = jnp.bfloat16
LANES = 128
STEP = 16


def remote(src, dst, send_sem, recv_sem, axis, target):
    return pltpu.make_async_remote_copy(
        src_ref=src, dst_ref=dst, send_sem=send_sem, recv_sem=recv_sem,
        device_id={axis: target}, device_id_type=MESH,
    )


def wait_bytes(ref, sem):
    pltpu.make_async_copy(ref, ref, sem).wait()


def toeplitz_rows(recv_h, toeplitz, chunk, blocks):
    rows = lax.broadcasted_iota(jnp.int32, (STEP, LANES), 0)
    lanes = lax.broadcasted_iota(jnp.int32, (STEP, LANES), 1)
    keep = [(lanes >= rows) & (lanes < LANES - STEP * part) for part in range(8)]
    per_step = 4

    def build(index, earlier):
        earlier = list(earlier)
        bases = {}
        for inner in range(per_step):
            lags = recv_h[chunk, per_step * index + inner].astype(F32)
            for row in range(4):
                bases[inner, row] = pltpu.roll(
                    jnp.broadcast_to(lags[row:row + 1, :], (STEP, LANES)), 0, 1,
                    stride=1, stride_axis=0).astype(BF16)
        for inner in range(per_step):
            for row in range(4):
                chan, half = row // 2, row % 2
                base = bases[inner, row]
                at = pl.multiple_of(256 * (per_step * index + inner) + LANES * half, LANES)
                for part in range(8):
                    mixed = jnp.where(keep[part], base, earlier[chan])
                    if part:
                        mixed = pltpu.roll(mixed, STEP * part, 1)
                    toeplitz[2 * chunk + chan, pl.ds(at + STEP * part, STEP), :] = mixed
                earlier[chan] = base
        return tuple(earlier)

    zero = jnp.zeros((STEP, LANES), BF16)
    lax.fori_loop(0, blocks // per_step, build, (zero, zero))


def kernel(
    ctx_n, ch_n,
    q_ref, k_ref, v_ref, taps_ref, sbias_ref, filt_ref, skip_ref, w_ref, obias_ref,
    out_ref,
    flat, halo_out, halo_in, wide, send_h, send_g, send_y, recv_h, recv_g, recv_y,
    gated_t, query_t, toeplitz, shifted, padded, acc, w_all, w_t, oper,
    send_sem, recv_sem, halo_sem, w_send, w_recv, o_send, o_recv, pass_send,
):
    me = lax.axis_index("ctx")
    my_ch = lax.axis_index("ch")
    other_core = 2 * (my_ch // 2) + 1 - lax.rem(my_ch, 2)

    barrier = pltpu.get_barrier_semaphore()

    @pl.loop(1, ctx_n)
    def _(step):
        pl.semaphore_signal(
            barrier, inc=1, device_id={"ctx": lax.rem(me + step, ctx_n)}, device_id_type=MESH)

    @pl.loop(1, ch_n)
    def _(step):
        pl.semaphore_signal(
            barrier, inc=1, device_id={"ch": lax.rem(my_ch + step, ch_n)}, device_id_type=MESH)

    def pack(chunk, halves, dst):
        for half in range(2):
            for chan in range(2):
                flat[pl.ds(2 * chan + half, 64, stride=4), :] = halves[half][
                    64 * chan:64 * chan + 64, :]
        dst[chunk] = flat[...].reshape(ctx_n, 4, LANES).astype(BF16)

    def unpack(chunk, src):
        flat[...] = src[chunk].astype(F32).reshape(4 * ctx_n, LANES)

    def exchange(src, dst, which, chunk):
        @pl.loop(1, ctx_n)
        def _(step):
            target = lax.rem(me + step, ctx_n)
            remote(src.at[chunk, target], dst.at[chunk, me], send_sem.at[which, chunk],
                   recv_sem.at[which, chunk], "ctx", target).start()
        dst[chunk, me] = src[chunk, me]

    def arrived(dst, which, chunk):
        wait_bytes(dst.at[chunk, pl.ds(0, ctx_n - 1)], recv_sem.at[which, chunk])

    cuts = [slice(0, LANES), slice(LANES, 2 * LANES)]

    for chunk in range(2):
        pack(chunk, [filt_ref[cut, cuts[chunk]].T for cut in cuts], send_h)

    tails = [ref[240:256, :].astype(F32)[14:16] for ref in (q_ref, k_ref, v_ref)]
    halo_out[...] = jnp.concatenate(tails + [jnp.zeros((10, 256), F32)], axis=0).astype(BF16)
    for index, ref in enumerate((q_ref, k_ref, v_ref)):
        wide[index, pl.ds(8, 256), :] = ref[...].astype(F32)

    pl.semaphore_wait(barrier, ctx_n + ch_n - 2)

    ahead = lax.rem(me + 1, ctx_n)
    halo_copy = remote(halo_out, halo_in, halo_sem.at[0], halo_sem.at[1], "ctx", ahead)
    halo_copy.start()
    for chunk in range(2):
        exchange(send_h, recv_h, 0, chunk)

    @pl.loop(1, ch_n)
    def _(step):
        target = lax.rem(my_ch + step, ch_n)
        remote(w_ref.at[:, pl.ds(pl.multiple_of(target * 256, 256), 256)], w_all.at[my_ch],
               w_send, w_recv, "ch", target).start()
    w_all[my_ch] = w_ref[:, pl.ds(pl.multiple_of(my_ch * 256, 256), 256)]

    halo_copy.wait()
    before = jnp.where(me > 0, halo_in[...].astype(F32), 0.0)
    for index in range(3):
        wide[index, 6:8, :] = before[2 * index:2 * index + 2, :]

    def short(index, half, chunk):
        at, cut = half * LANES, cuts[chunk]
        return (
            taps_ref[index, 0:1, cut] * wide[index, pl.ds(6 + at, LANES), cut]
            + taps_ref[index, 1:2, cut] * wide[index, pl.ds(7 + at, LANES), cut]
            + taps_ref[index, 2:3, cut] * wide[index, pl.ds(8 + at, LANES), cut]
            + sbias_ref[index:index + 1, cut]
        )

    for chunk in range(2):
        for half in range(2):
            gated_t[chunk, half] = (short(1, half, chunk) * short(2, half, chunk)).T
        pack(chunk, [gated_t[chunk, 0], gated_t[chunk, 1]], send_g)
        exchange(send_g, recv_g, 1, chunk)

    for chunk in range(2):
        for half in range(2):
            query_t[chunk, half] = short(0, half, chunk).T

    for chunk in range(2):
        arrived(recv_h, 0, chunk)
        toeplitz_rows(recv_h, toeplitz, chunk, ctx_n)

    padded[0:STEP, :] = jnp.zeros((STEP, LANES), F32)
    for chunk in range(2):
        arrived(recv_g, 1, chunk)
        unpack(chunk, recv_g)
        for chan in range(2):
            for half in range(2):
                padded[pl.ds(STEP + half, 64, stride=2), :] = flat[
                    pl.ds(2 * chan + half, 64, stride=4), :]
            for lag in range(STEP):
                shifted[:, pl.ds(lag * LANES, LANES)] = padded[
                    pl.ds(STEP - lag, LANES), :].astype(BF16)
            for part in range(8):
                rows = LANES - STEP * part
                product = jnp.dot(
                    shifted[0:rows, :],
                    toeplitz[2 * chunk + chan, pl.ds(2048 * part, 2048), :],
                    preferred_element_type=F32)
                if part == 0:
                    acc[...] = product
                else:
                    acc[pl.ds(STEP * part, rows), :] += product
            for half in range(2):
                flat[pl.ds(2 * chan + half, 64, stride=4), :] = acc[pl.ds(half, 64, stride=2), :]
        send_y[chunk] = flat[...].reshape(ctx_n, 4, LANES).astype(BF16)
        exchange(send_y, recv_y, 2, chunk)

    wait_bytes(w_all.at[pl.ds(0, ch_n - 1)], w_recv)

    @pl.loop(0, ch_n)
    def _(index):
        for chunk in range(2):
            w_t[index, chunk] = w_all[index, cuts[chunk], :].T

    def pass_on(source, chunk, copy_sem, target):
        return remote(oper.at[source, chunk], oper.at[source, chunk], copy_sem,
                      o_recv.at[source, chunk], "ch", target)

    for chunk in range(2):
        skip_t = jnp.broadcast_to(skip_ref[:, cuts[chunk]], (LANES, LANES)).T
        arrived(recv_y, 2, chunk)
        unpack(chunk, recv_y)
        for half in range(2):
            conv = jnp.concatenate(
                [flat[pl.ds(2 * chan + half, 64, stride=4), :] for chan in range(2)], axis=0)
            oper[my_ch, chunk, :, cuts[half]] = (
                query_t[chunk, half] * (conv + skip_t * gated_t[chunk, half])).astype(BF16)
        for hop in (2, 6, 4):
            pass_on(my_ch, chunk, o_send, lax.rem(my_ch + hop, ch_n)).start()
        pass_on(my_ch, chunk, o_send, other_core).start()

    bias_t = jnp.broadcast_to(obias_ref[...], (LANES, 256)).T
    total = jnp.concatenate([bias_t, bias_t], axis=1)

    def add(total, source, chunk):
        return total + jnp.dot(w_t[source, chunk], oper[source, chunk], preferred_element_type=F32)

    for chunk in range(2):
        total = add(total, my_ch, chunk)
    for chunk in range(2):
        for hop in (2, 6, 4):
            source = lax.rem(my_ch + hop, ch_n)
            wait_bytes(oper.at[source, chunk], o_recv.at[source, chunk])
            pass_on(source, chunk, pass_send, other_core).start()
            total = add(total, source, chunk)
        for hop in (0, 2, 6, 4):
            source = lax.rem(other_core + hop, ch_n)
            wait_bytes(oper.at[source, chunk], o_recv.at[source, chunk])
            total = add(total, source, chunk)
    out_ref[...] = total.astype(BF16)

    for which, ref in enumerate((send_h, send_g, send_y)):
        for chunk in range(2):
            wait_bytes(ref.at[chunk, pl.ds(0, ctx_n - 1)], send_sem.at[which, chunk])
    wait_bytes(w_all.at[pl.ds(0, ch_n - 1)], w_send)
    wait_bytes(oper.at[pl.ds(0, 4)], o_send)
    wait_bytes(oper.at[pl.ds(0, 3)], pass_send)


def shards(q, k, v, taps, sbias, filt, skip, weight, obias):
    ctx_n, ch_n = lax.axis_size("ctx"), lax.axis_size("ch")
    vmem = pl.BlockSpec(memory_space=pltpu.VMEM)
    message = pltpu.VMEM((2, ctx_n, 4, LANES), BF16)
    dma = pltpu.SemaphoreType.DMA
    return pl.pallas_call(
        functools.partial(kernel, ctx_n, ch_n),
        out_shape=jax.ShapeDtypeStruct((256, 256), BF16),
        in_specs=[vmem] * 9,
        out_specs=vmem,
        scratch_shapes=[
            pltpu.VMEM((256, LANES), F32),
            pltpu.VMEM((16, 256), BF16),
            pltpu.VMEM((16, 256), BF16),
            pltpu.VMEM((3, 264, 256), F32),
            message, message, message, message, message, message,
            pltpu.VMEM((2, 2, LANES, LANES), F32),
            pltpu.VMEM((2, 2, LANES, LANES), F32),
            pltpu.VMEM((4, 16384, LANES), BF16),
            pltpu.VMEM((LANES, 2048), BF16),
            pltpu.VMEM((LANES + STEP, LANES), F32),
            pltpu.VMEM((LANES, LANES), F32),
            pltpu.VMEM((ch_n, 256, 256), BF16),
            pltpu.VMEM((ch_n, 2, 256, LANES), BF16),
            pltpu.VMEM((ch_n, 2, LANES, 256), BF16),
            dma((3, 2)), dma((3, 2)), dma((2,)), dma, dma, dma, dma((ch_n, 2)), dma,
        ],
        compiler_params=pltpu.CompilerParams(
            collective_id=3, has_side_effects=True, vmem_limit_bytes=50 * 2**20),
    )(q, k, v, taps, sbias, filt, skip.reshape(1, -1), weight, obias.reshape(1, -1))


def solution(mesh):
    return jax.shard_map(
        shards,
        mesh=mesh,
        in_specs=(
            P("ctx", "ch"),
            P("ctx", "ch"),
            P("ctx", "ch"),
            P(None, None, "ch"),
            P(None, "ch"),
            P("ctx", "ch"),
            P("ch"),
            P("ch", None),
            P("ch"),
        ),
        out_specs=P("ch", "ctx"),
        check_vma=False,
    )
```

time: 89.8 us -> 66.4 us (0.74)
  Pallas kernels: 81.8 us -> 58.4 us
    pallas_call x1, Pallas kernels: 81.8 us -> 58.4 us  [shards(): pl.pallas_call(functools.partial(kernel, ctx_n, ch_n), out_shape=jax.Shap...]
where the time goes in v2:
time: 66.4 us; the launch traced here: 66.1 us
  Pallas kernels  58.4 us (88%)
  local copies, waits for them, and re-layouts  7.63 us (11%)
    pallas_call x1, Pallas kernels, shards(): pl.pallas_call(functools.partial(kernel, ctx_n, ch_n), out_shape=jax.Shap...  58.4 us
    unnamed x19, local copies, waits for them, and re-layouts  7.63 us

profile of v2, /device:TPU:1, one launch (start us, length us, event | category | flops | bytes accessed | tf_op | source)
XLA Modules:
  0.0 66.1 jit_solution(11437044455310052633)
XLA Ops:
  0.0 0.0 copy-start.8
  0.0 0.0 copy-start.7
  0.0 0.7 %copy-done.8 = f32[256]{0:T(256)S(1)} copy-done((f32[256]{0:T(256)S(1)}, f32[256]{0:T(256)}, u32[]{:S(2)}) %copy-start.8) | copy-done | bytes 1048
  0.7 0.0 copy-done.7
  0.7 0.0 copy-start
  0.7 1.2 %copy-done = bf16[256,2048]{1,0:T(8,128)(2,1)S(1)} copy-done((bf16[256,2048]{1,0:T(8,128)(2,1)S(1)}, bf16[256,2048]{1,0:T(8,128)(2,1)}, u32[]{:S(2)}) %copy-start) | copy-done | bytes 1048600
  1.9 0.0 copy-start.1
  1.9 0.9 %copy-done.1 = f32[256,256]{1,0:T(8,128)S(1)} copy-done((f32[256,256]{1,0:T(8,128)S(1)}, f32[256,256]{1,0:T(8,128)}, u32[]{:S(2)}) %copy-start.1) | copy-done | bytes 262168
  2.9 0.0 copy-start.2
  2.9 0.9 %copy-done.2 = bf16[256,256]{1,0:T(8,128)(2,1)S(1)} copy-done((bf16[256,256]{1,0:T(8,128)(2,1)S(1)}, bf16[256,256]{1,0:T(8,128)(2,1)}, u32[]{:S(2)}) %copy-start.2) | copy-done | bytes 131096
  3.8 0.0 copy-start.3
  3.8 0.9 %copy-done.3 = bf16[256,256]{1,0:T(8,128)(2,1)S(1)} copy-done((bf16[256,256]{1,0:T(8,128)(2,1)S(1)}, bf16[256,256]{1,0:T(8,128)(2,1)}, u32[]{:S(2)}) %copy-start.3) | copy-done | bytes 131096
  4.7 0.0 copy-start.4
  4.7 0.9 %copy-done.4 = bf16[256,256]{1,0:T(8,128)(2,1)S(1)} copy-done((bf16[256,256]{1,0:T(8,128)(2,1)S(1)}, bf16[256,256]{1,0:T(8,128)(2,1)}, u32[]{:S(2)}) %copy-start.4) | copy-done | bytes 131096
  5.6 0.0 copy-start.5
  5.6 0.7 %copy-done.5 = f32[3,3,256]{2,1,0:T(4,128)S(1)} copy-done((f32[3,3,256]{2,1,0:T(4,128)S(1)}, f32[3,3,256]{2,1,0:T(4,128)}, u32[]{:S(2)}) %copy-start.5) | copy-done | bytes 9240
  6.3 0.0 copy-start.6
  6.3 0.7 %copy-done.6 = f32[3,256]{1,0:T(4,128)S(1)} copy-done((f32[3,256]{1,0:T(4,128)S(1)}, f32[3,256]{1,0:T(4,128)}, u32[]{:S(2)}) %copy-start.6) | copy-done | bytes 3096
  7.0 58.4 %shard_map.91 = bf16[256,256]{1,0:T(8,128)(2,1)S(1)} custom-call(bf16[256,256]{1,0:T(8,128)(2,1)S(1)} %copy-done.2, bf16[256,256]{1,0:T(8,128)(2,1)S(1)} %copy-done.3, bf16[256,256]{1,0:T(8,128)(2,1)S(1)} %copy-done.4, f32[3,3,256]{2,1,0:T(4,128)S(1)} %copy-done.5, f32[3,256]{1,0:T(4,128)S(1)} %copy-done.6, f32[256,256]{1,0:T(8,128)S(1)} %copy-done.1, ...), custom_call_target="tpu_custom_call" | custom-call | tf_op jit(solution)/shard_map/pallas_call | solution.py:241
  65.4 0.7 copy.11
Async XLA Ops:
  0.0 0.7 %copy-start.8 = (f32[256]{0:T(256)S(1)}, f32[256]{0:T(256)}, u32[]{:S(2)}) copy-start(f32[256]{0:T(256)} %param.17) | copy-start | bytes 3076
  0.0 0.7 %copy-start.7 = (f32[256]{0:T(256)S(1)}, f32[256]{0:T(256)}, u32[]{:S(2)}) copy-start(f32[256]{0:T(256)} %param.15) | copy-start | bytes 3076
  0.7 1.2 %copy-start = (bf16[256,2048]{1,0:T(8,128)(2,1)S(1)}, bf16[256,2048]{1,0:T(8,128)(2,1)}, u32[]{:S(2)}) copy-start(bf16[256,2048]{1,0:T(8,128)(2,1)} %w_ref.1) | copy-start | bytes 3145732
  1.9 0.9 %copy-start.1 = (f32[256,256]{1,0:T(8,128)S(1)}, f32[256,256]{1,0:T(8,128)}, u32[]{:S(2)}) copy-start(f32[256,256]{1,0:T(8,128)} %filt_ref.1) | copy-start | bytes 786436
  2.9 0.9 %copy-start.2 = (bf16[256,256]{1,0:T(8,128)(2,1)S(1)}, bf16[256,256]{1,0:T(8,128)(2,1)}, u32[]{:S(2)}) copy-start(bf16[256,256]{1,0:T(8,128)(2,1)} %q_ref.1) | copy-start | bytes 393220
  3.8 0.9 %copy-start.3 = (bf16[256,256]{1,0:T(8,128)(2,1)S(1)}, bf16[256,256]{1,0:T(8,128)(2,1)}, u32[]{:S(2)}) copy-start(bf16[256,256]{1,0:T(8,128)(2,1)} %k_ref.1) | copy-start | bytes 393220
  4.7 0.9 %copy-start.4 = (bf16[256,256]{1,0:T(8,128)(2,1)S(1)}, bf16[256,256]{1,0:T(8,128)(2,1)}, u32[]{:S(2)}) copy-start(bf16[256,256]{1,0:T(8,128)(2,1)} %v_ref.1) | copy-start | bytes 393220
  5.6 0.7 %copy-start.5 = (f32[3,3,256]{2,1,0:T(4,128)S(1)}, f32[3,3,256]{2,1,0:T(4,128)}, u32[]{:S(2)}) copy-start(f32[3,3,256]{2,1,0:T(4,128)} %taps_ref.1) | copy-start | bytes 27652
  6.3 0.7 %copy-start.6 = (f32[3,256]{1,0:T(4,128)S(1)}, f32[3,256]{1,0:T(4,128)}, u32[]{:S(2)}) copy-start(f32[3,256]{1,0:T(4,128)} %sbias_ref.1) | copy-start | bytes 9220

commit v3 on v2

--- a/solution.py
+++ b/solution.py
@@ -12,6 +12,7 @@
 BF16 = jnp.bfloat16
 LANES = 128
 STEP = 16
+PHASE = 32
 
 
 def remote(src, dst, send_sem, recv_sem, axis, target):
@@ -28,8 +29,9 @@
 def toeplitz_rows(recv_h, toeplitz, chunk, blocks):
     rows = lax.broadcasted_iota(jnp.int32, (STEP, LANES), 0)
     lanes = lax.broadcasted_iota(jnp.int32, (STEP, LANES), 1)
-    keep = [(lanes >= rows) & (lanes < LANES - STEP * part) for part in range(8)]
-    per_step = 4
+    parts = PHASE // STEP
+    keep = [(lanes >= rows) & (lanes < LANES - STEP * part) for part in range(parts)]
+    per_step = 8
 
     def build(index, earlier):
         earlier = list(earlier)
@@ -44,8 +46,8 @@
             for row in range(4):
                 chan, half = row // 2, row % 2
                 base = bases[inner, row]
-                at = pl.multiple_of(256 * (per_step * index + inner) + LANES * half, LANES)
-                for part in range(8):
+                at = pl.multiple_of(PHASE * (2 * (per_step * index + inner) + half), PHASE)
+                for part in range(parts):
                     mixed = jnp.where(keep[part], base, earlier[chan])
                     if part:
                         mixed = pltpu.roll(mixed, STEP * part, 1)
@@ -57,17 +59,62 @@
     lax.fori_loop(0, blocks // per_step, build, (zero, zero))
 
 
+def channel_conv(blocks, phases, shifted, acc, toeplitz, chan):
+    group = lax.broadcasted_iota(jnp.int32, (LANES, LANES), 1) // PHASE
+    count = LANES // PHASE
+    for turn in range(1, count):
+        blocks[turn, pl.ds(STEP, LANES), :] = pltpu.roll(
+            blocks[0, pl.ds(STEP, LANES), :], PHASE * turn, 1)
+    for phase in range(count):
+        value = blocks[(-phase) % count, pl.ds(STEP, LANES), :]
+        for lag in range(1, count):
+            value = jnp.where(
+                group == lag, blocks[(lag - phase) % count, pl.ds(STEP - lag, LANES), :], value)
+        phases[phase, pl.ds(STEP, LANES), :] = value
+        for quad in range(STEP // count):
+            shifted[phase, :, quad * LANES:(quad + 1) * LANES] = phases[
+                phase, pl.ds(STEP - count * quad, LANES), :].astype(BF16)
+    depth = STEP * PHASE
+    for part in range(LANES // STEP):
+        rows = LANES - STEP * part
+        product = jnp.dot(
+            shifted[:, 0:rows, :].reshape(count * rows, depth),
+            toeplitz[chan, pl.ds(depth * part, depth), :],
+            preferred_element_type=F32).reshape(count, rows, LANES)
+        if part == 0:
+            acc[:, pl.ds(8, LANES), :] = product
+        else:
+            acc[:, pl.ds(8 + STEP * part, rows), :] += product
+    value = acc[0, pl.ds(8, LANES), :]
+    for phase in range(1, count):
+        value = value + pltpu.roll(
+            jnp.where(group < count - phase, acc[phase, pl.ds(8, LANES), :],
+                      acc[phase, pl.ds(7, LANES), :]), PHASE * phase, 1)
+    return value
+
+
 def kernel(
     ctx_n, ch_n,
-    q_ref, k_ref, v_ref, taps_ref, sbias_ref, filt_ref, skip_ref, w_ref, obias_ref,
+    q_hbm, k_hbm, v_hbm, taps_hbm, sbias_hbm, filt_hbm, skip_hbm, w_ref, obias_hbm,
     out_ref,
+    q_ref, k_ref, v_ref, taps_ref, sbias_ref, filt_ref, skip_ref, obias_ref,
     flat, halo_out, halo_in, wide, send_h, send_g, send_y, recv_h, recv_g, recv_y,
-    gated_t, query_t, toeplitz, shifted, padded, acc, w_all, w_t, oper,
-    send_sem, recv_sem, halo_sem, w_send, w_recv, o_send, o_recv, pass_send,
+    gated_t, query_t, toeplitz, shifted, blocks, phases, result, acc, w_all, w_t, oper,
+    send_sem, recv_sem, halo_sem, w_send, w_recv, o_send, o_recv, pass_send, in_sem,
 ):
     me = lax.axis_index("ctx")
     my_ch = lax.axis_index("ch")
     other_core = 2 * (my_ch // 2) + 1 - lax.rem(my_ch, 2)
+
+    fetches = [
+        pltpu.make_async_copy(src, dst, in_sem.at[index])
+        for index, (src, dst) in enumerate((
+            (filt_hbm, filt_ref), (q_hbm, q_ref), (k_hbm, k_ref), (v_hbm, v_ref),
+            (taps_hbm, taps_ref), (sbias_hbm, sbias_ref), (skip_hbm, skip_ref),
+            (obias_hbm, obias_ref),
+            (w_ref.at[:, pl.ds(pl.multiple_of(my_ch * 256, 256), 256)], w_all.at[my_ch])))
+    ]
+    fetches[0].start()
 
     barrier = pltpu.get_barrier_semaphore()
 
@@ -104,9 +151,19 @@
 
     cuts = [slice(0, LANES), slice(LANES, 2 * LANES)]
 
+    for fetch in fetches[1:]:
+        fetch.start()
+    for count in range(LANES // PHASE):
+        blocks[count, 0:STEP, :] = jnp.zeros((STEP, LANES), F32)
+        phases[count, 0:STEP, :] = jnp.zeros((STEP, LANES), F32)
+        acc[count, 0:8, :] = jnp.zeros((8, LANES), F32)
+
+    fetches[0].wait()
     for chunk in range(2):
         pack(chunk, [filt_ref[cut, cuts[chunk]].T for cut in cuts], send_h)
 
+    for fetch in fetches[1:]:
+        fetch.wait()
     tails = [ref[240:256, :].astype(F32)[14:16] for ref in (q_ref, k_ref, v_ref)]
     halo_out[...] = jnp.concatenate(tails + [jnp.zeros((10, 256), F32)], axis=0).astype(BF16)
     for index, ref in enumerate((q_ref, k_ref, v_ref)):
@@ -125,7 +182,6 @@
         target = lax.rem(my_ch + step, ch_n)
         remote(w_ref.at[:, pl.ds(pl.multiple_of(target * 256, 256), 256)], w_all.at[my_ch],
                w_send, w_recv, "ch", target).start()
-    w_all[my_ch] = w_ref[:, pl.ds(pl.multiple_of(my_ch * 256, 256), 256)]
 
     halo_copy.wait()
     before = jnp.where(me > 0, halo_in[...].astype(F32), 0.0)
@@ -148,38 +204,24 @@
         exchange(send_g, recv_g, 1, chunk)
 
     for chunk in range(2):
-        for half in range(2):
-            query_t[chunk, half] = short(0, half, chunk).T
-
-    for chunk in range(2):
         arrived(recv_h, 0, chunk)
         toeplitz_rows(recv_h, toeplitz, chunk, ctx_n)
-
-    padded[0:STEP, :] = jnp.zeros((STEP, LANES), F32)
-    for chunk in range(2):
         arrived(recv_g, 1, chunk)
         unpack(chunk, recv_g)
         for chan in range(2):
             for half in range(2):
-                padded[pl.ds(STEP + half, 64, stride=2), :] = flat[
+                blocks[0, pl.ds(STEP + half, 64, stride=2), :] = flat[
                     pl.ds(2 * chan + half, 64, stride=4), :]
-            for lag in range(STEP):
-                shifted[:, pl.ds(lag * LANES, LANES)] = padded[
-                    pl.ds(STEP - lag, LANES), :].astype(BF16)
-            for part in range(8):
-                rows = LANES - STEP * part
-                product = jnp.dot(
-                    shifted[0:rows, :],
-                    toeplitz[2 * chunk + chan, pl.ds(2048 * part, 2048), :],
-                    preferred_element_type=F32)
-                if part == 0:
-                    acc[...] = product
-                else:
-                    acc[pl.ds(STEP * part, rows), :] += product
+            result[...] = channel_conv(
+                blocks, phases, shifted, acc, toeplitz, 2 * chunk + chan)
             for half in range(2):
-                flat[pl.ds(2 * chan + half, 64, stride=4), :] = acc[pl.ds(half, 64, stride=2), :]
+                flat[pl.ds(2 * chan + half, 64, stride=4), :] = result[pl.ds(half, 64, stride=2), :]
         send_y[chunk] = flat[...].reshape(ctx_n, 4, LANES).astype(BF16)
         exchange(send_y, recv_y, 2, chunk)
+
+    for chunk in range(2):
+        for half in range(2):
+            query_t[chunk, half] = short(0, half, chunk).T
 
     wait_bytes(w_all.at[pl.ds(0, ch_n - 1)], w_recv)
 
@@ -241,9 +283,17 @@
     return pl.pallas_call(
         functools.partial(kernel, ctx_n, ch_n),
         out_shape=jax.ShapeDtypeStruct((256, 256), BF16),
-        in_specs=[vmem] * 9,
+        in_specs=[pl.BlockSpec(memory_space=pl.ANY)] * 9,
         out_specs=vmem,
         scratch_shapes=[
+            pltpu.VMEM((256, 256), BF16),
+            pltpu.VMEM((256, 256), BF16),
+            pltpu.VMEM((256, 256), BF16),
+            pltpu.VMEM((3, 3, 256), F32),
+            pltpu.VMEM((3, 256), F32),
+            pltpu.VMEM((256, 256), F32),
+            pltpu.VMEM((1, 256), F32),
+            pltpu.VMEM((1, 256), F32),
             pltpu.VMEM((256, LANES), F32),
             pltpu.VMEM((16, 256), BF16),
             pltpu.VMEM((16, 256), BF16),
@@ -251,17 +301,19 @@
             message, message, message, message, message, message,
             pltpu.VMEM((2, 2, LANES, LANES), F32),
             pltpu.VMEM((2, 2, LANES, LANES), F32),
-            pltpu.VMEM((4, 16384, LANES), BF16),
-            pltpu.VMEM((LANES, 2048), BF16),
-            pltpu.VMEM((LANES + STEP, LANES), F32),
+            pltpu.VMEM((4, LANES * PHASE, LANES), BF16),
+            pltpu.VMEM((LANES // PHASE, LANES, STEP * PHASE), BF16),
+            pltpu.VMEM((LANES // PHASE, STEP + LANES, LANES), F32),
+            pltpu.VMEM((LANES // PHASE, STEP + LANES, LANES), F32),
             pltpu.VMEM((LANES, LANES), F32),
+            pltpu.VMEM((LANES // PHASE, 8 + LANES, LANES), F32),
             pltpu.VMEM((ch_n, 256, 256), BF16),
             pltpu.VMEM((ch_n, 2, 256, LANES), BF16),
             pltpu.VMEM((ch_n, 2, LANES, 256), BF16),
-            dma((3, 2)), dma((3, 2)), dma((2,)), dma, dma, dma, dma((ch_n, 2)), dma,
+            dma((3, 2)), dma((3, 2)), dma((2,)), dma, dma, dma, dma((ch_n, 2)), dma, dma((9,)),
         ],
         compiler_params=pltpu.CompilerParams(
-            collective_id=3, has_side_effects=True, vmem_limit_bytes=50 * 2**20),
+            collective_id=3, has_side_effects=True, vmem_limit_bytes=63 * 2**20),
     )(q, k, v, taps, sbias, filt, skip.reshape(1, -1), weight, obias.reshape(1, -1))
 
 

time: 66.4 us -> 59.1 us (0.89)
  local copies, waits for them, and re-layouts: 7.63 us -> 1.57 us
  Pallas kernels: 58.4 us -> 57.4 us
    unnamed x19 -> x1, local copies, waits for them, and re-layouts: 7.63 us -> 1.57 us
    pallas_call x1, Pallas kernels: 58.4 us -> 57.4 us  [shards(): pl.pallas_call(functools.partial(kernel, ctx_n, ch_n), out_shape=jax.Shap...]
where the time goes in v3:
time: 59.1 us; the launch traced here: 59 us
  Pallas kernels  57.4 us (97%)
  local copies, waits for them, and re-layouts  1.57 us (3%)
    pallas_call x1, Pallas kernels, shards(): pl.pallas_call(functools.partial(kernel, ctx_n, ch_n), out_shape=jax.Shap...  57.4 us
    unnamed x1, local copies, waits for them, and re-layouts  1.57 us

profile of v3, /device:TPU:1, one launch (start us, length us, event | category | flops | bytes accessed | tf_op | source)
XLA Modules:
  0.0 59.0 jit_solution(10417798074726131198)
XLA Ops:
  0.0 57.4 %shard_map.91 = bf16[256,256]{1,0:T(8,128)(2,1)} custom-call(bf16[256,256]{1,0:T(8,128)(2,1)} %q_hbm.1, bf16[256,256]{1,0:T(8,128)(2,1)} %k_hbm.1, bf16[256,256]{1,0:T(8,128)(2,1)} %v_hbm.1, f32[3,3,256]{2,1,0:T(4,128)} %taps_hbm.1, f32[3,256]{1,0:T(4,128)} %sbias_hbm.1, f32[256,256]{1,0:T(8,128)} %filt_hbm.1, f32[1,256]{1,0:T(1,128)} %bitcast.2, ...), custom_call_target="tpu_custom_call" | custom-call | tf_op jit(solution)/shard_map/pallas_call | solution.py:283
  57.4 1.6 %copy.11 = bf16[256,256]{1,0:T(8,128)(2,1)} copy(bf16[256,256]{1,0:T(8,128)(2,1)} %shard_map.91) | data formatting | bytes 262144

commit v4 on v3

--- a/solution.py
+++ b/solution.py
@@ -26,24 +26,24 @@
     pltpu.make_async_copy(ref, ref, sem).wait()
 
 
-def toeplitz_rows(recv_h, toeplitz, chunk, blocks):
+def toeplitz_rows(recv_h, toeplitz, blocks):
     rows = lax.broadcasted_iota(jnp.int32, (STEP, LANES), 0)
     lanes = lax.broadcasted_iota(jnp.int32, (STEP, LANES), 1)
     parts = PHASE // STEP
     keep = [(lanes >= rows) & (lanes < LANES - STEP * part) for part in range(parts)]
-    per_step = 8
+    per_step = 4
 
     def build(index, earlier):
         earlier = list(earlier)
         bases = {}
         for inner in range(per_step):
-            lags = recv_h[chunk, per_step * index + inner].astype(F32)
-            for row in range(4):
+            lags = recv_h[per_step * index + inner].astype(F32)
+            for row in range(8):
                 bases[inner, row] = pltpu.roll(
                     jnp.broadcast_to(lags[row:row + 1, :], (STEP, LANES)), 0, 1,
                     stride=1, stride_axis=0).astype(BF16)
         for inner in range(per_step):
-            for row in range(4):
+            for row in range(8):
                 chan, half = row // 2, row % 2
                 base = bases[inner, row]
                 at = pl.multiple_of(PHASE * (2 * (per_step * index + inner) + half), PHASE)
@@ -51,12 +51,12 @@
                     mixed = jnp.where(keep[part], base, earlier[chan])
                     if part:
                         mixed = pltpu.roll(mixed, STEP * part, 1)
-                    toeplitz[2 * chunk + chan, pl.ds(at + STEP * part, STEP), :] = mixed
+                    toeplitz[chan, pl.ds(at + STEP * part, STEP), :] = mixed
                 earlier[chan] = base
         return tuple(earlier)
 
     zero = jnp.zeros((STEP, LANES), BF16)
-    lax.fori_loop(0, blocks // per_step, build, (zero, zero))
+    lax.fori_loop(0, blocks // per_step, build, (zero,) * 4)
 
 
 def channel_conv(blocks, phases, shifted, acc, toeplitz, chan):
@@ -98,9 +98,9 @@
     q_hbm, k_hbm, v_hbm, taps_hbm, sbias_hbm, filt_hbm, skip_hbm, w_ref, obias_hbm,
     out_ref,
     q_ref, k_ref, v_ref, taps_ref, sbias_ref, filt_ref, skip_ref, obias_ref,
-    flat, halo_out, halo_in, wide, send_h, send_g, send_y, recv_h, recv_g, recv_y,
+    flat, wide_flat, halo_out, halo_in, wide, send_h, send_g, send_y, recv_h, recv_g, recv_y,
     gated_t, query_t, toeplitz, shifted, blocks, phases, result, acc, w_all, w_t, oper,
-    send_sem, recv_sem, halo_sem, w_send, w_recv, o_send, o_recv, pass_send, in_sem,
+    send_sem, recv_sem, halo_sem, w_send, w_recv, o_send, o_recv, in_sem, h_sem,
 ):
     me = lax.axis_index("ctx")
     my_ch = lax.axis_index("ch")
@@ -159,23 +159,29 @@
         acc[count, 0:8, :] = jnp.zeros((8, LANES), F32)
 
     fetches[0].wait()
-    for chunk in range(2):
-        pack(chunk, [filt_ref[cut, cuts[chunk]].T for cut in cuts], send_h)
+    for half in range(2):
+        columns = filt_ref[cuts[half], :].T
+        for chan in range(4):
+            wide_flat[pl.ds(2 * chan + half, 64, stride=8), :] = columns[
+                64 * chan:64 * chan + 64, :]
+    send_h[...] = wide_flat[...].reshape(ctx_n, 8, LANES).astype(BF16)
 
     for fetch in fetches[1:]:
         fetch.wait()
-    tails = [ref[240:256, :].astype(F32)[14:16] for ref in (q_ref, k_ref, v_ref)]
+    tails = [ref[240:256, :].astype(F32)[14:16] for ref in (k_ref, v_ref, q_ref)]
     halo_out[...] = jnp.concatenate(tails + [jnp.zeros((10, 256), F32)], axis=0).astype(BF16)
-    for index, ref in enumerate((q_ref, k_ref, v_ref)):
-        wide[index, pl.ds(8, 256), :] = ref[...].astype(F32)
 
     pl.semaphore_wait(barrier, ctx_n + ch_n - 2)
 
     ahead = lax.rem(me + 1, ctx_n)
     halo_copy = remote(halo_out, halo_in, halo_sem.at[0], halo_sem.at[1], "ctx", ahead)
     halo_copy.start()
-    for chunk in range(2):
-        exchange(send_h, recv_h, 0, chunk)
+
+    @pl.loop(1, ctx_n)
+    def _(step):
+        target = lax.rem(me + step, ctx_n)
+        remote(send_h.at[target], recv_h.at[me], h_sem.at[0], h_sem.at[1], "ctx", target).start()
+    recv_h[me] = send_h[me]
 
     @pl.loop(1, ch_n)
     def _(step):
@@ -183,17 +189,19 @@
         remote(w_ref.at[:, pl.ds(pl.multiple_of(target * 256, 256), 256)], w_all.at[my_ch],
                w_send, w_recv, "ch", target).start()
 
+    for index, ref in enumerate((k_ref, v_ref, q_ref)):
+        wide[index, pl.ds(8, 256), :] = ref[...].astype(F32)
     halo_copy.wait()
     before = jnp.where(me > 0, halo_in[...].astype(F32), 0.0)
     for index in range(3):
         wide[index, 6:8, :] = before[2 * index:2 * index + 2, :]
 
     def short(index, half, chunk):
-        at, cut = half * LANES, cuts[chunk]
+        at, cut, slot = half * LANES, cuts[chunk], (index + 2) % 3
         return (
-            taps_ref[index, 0:1, cut] * wide[index, pl.ds(6 + at, LANES), cut]
-            + taps_ref[index, 1:2, cut] * wide[index, pl.ds(7 + at, LANES), cut]
-            + taps_ref[index, 2:3, cut] * wide[index, pl.ds(8 + at, LANES), cut]
+            taps_ref[index, 0:1, cut] * wide[slot, pl.ds(6 + at, LANES), cut]
+            + taps_ref[index, 1:2, cut] * wide[slot, pl.ds(7 + at, LANES), cut]
+            + taps_ref[index, 2:3, cut] * wide[slot, pl.ds(8 + at, LANES), cut]
             + sbias_ref[index:index + 1, cut]
         )
 
@@ -201,12 +209,12 @@
         for half in range(2):
             gated_t[chunk, half] = (short(1, half, chunk) * short(2, half, chunk)).T
         pack(chunk, [gated_t[chunk, 0], gated_t[chunk, 1]], send_g)
-        exchange(send_g, recv_g, 1, chunk)
-
-    for chunk in range(2):
-        arrived(recv_h, 0, chunk)
-        toeplitz_rows(recv_h, toeplitz, chunk, ctx_n)
-        arrived(recv_g, 1, chunk)
+        exchange(send_g, recv_g, 0, chunk)
+
+    wait_bytes(recv_h.at[pl.ds(0, ctx_n - 1)], h_sem.at[1])
+    toeplitz_rows(recv_h, toeplitz, ctx_n)
+    for chunk in range(2):
+        arrived(recv_g, 0, chunk)
         unpack(chunk, recv_g)
         for chan in range(2):
             for half in range(2):
@@ -217,7 +225,7 @@
             for half in range(2):
                 flat[pl.ds(2 * chan + half, 64, stride=4), :] = result[pl.ds(half, 64, stride=2), :]
         send_y[chunk] = flat[...].reshape(ctx_n, 4, LANES).astype(BF16)
-        exchange(send_y, recv_y, 2, chunk)
+        exchange(send_y, recv_y, 1, chunk)
 
     for chunk in range(2):
         for half in range(2):
@@ -236,16 +244,15 @@
 
     for chunk in range(2):
         skip_t = jnp.broadcast_to(skip_ref[:, cuts[chunk]], (LANES, LANES)).T
-        arrived(recv_y, 2, chunk)
+        arrived(recv_y, 1, chunk)
         unpack(chunk, recv_y)
         for half in range(2):
             conv = jnp.concatenate(
                 [flat[pl.ds(2 * chan + half, 64, stride=4), :] for chan in range(2)], axis=0)
             oper[my_ch, chunk, :, cuts[half]] = (
                 query_t[chunk, half] * (conv + skip_t * gated_t[chunk, half])).astype(BF16)
-        for hop in (2, 6, 4):
+        for hop in (4, 3, 5, 2, 6, 1, 7):
             pass_on(my_ch, chunk, o_send, lax.rem(my_ch + hop, ch_n)).start()
-        pass_on(my_ch, chunk, o_send, other_core).start()
 
     bias_t = jnp.broadcast_to(obias_ref[...], (LANES, 256)).T
     total = jnp.concatenate([bias_t, bias_t], axis=1)
@@ -256,23 +263,18 @@
     for chunk in range(2):
         total = add(total, my_ch, chunk)
     for chunk in range(2):
-        for hop in (2, 6, 4):
+        for hop in (1, 7, 2, 6, 3, 5, 4):
             source = lax.rem(my_ch + hop, ch_n)
-            wait_bytes(oper.at[source, chunk], o_recv.at[source, chunk])
-            pass_on(source, chunk, pass_send, other_core).start()
-            total = add(total, source, chunk)
-        for hop in (0, 2, 6, 4):
-            source = lax.rem(other_core + hop, ch_n)
             wait_bytes(oper.at[source, chunk], o_recv.at[source, chunk])
             total = add(total, source, chunk)
     out_ref[...] = total.astype(BF16)
 
-    for which, ref in enumerate((send_h, send_g, send_y)):
+    wait_bytes(send_h.at[pl.ds(0, ctx_n - 1)], h_sem.at[0])
+    for which, ref in enumerate((send_g, send_y)):
         for chunk in range(2):
             wait_bytes(ref.at[chunk, pl.ds(0, ctx_n - 1)], send_sem.at[which, chunk])
     wait_bytes(w_all.at[pl.ds(0, ch_n - 1)], w_send)
-    wait_bytes(oper.at[pl.ds(0, 4)], o_send)
-    wait_bytes(oper.at[pl.ds(0, 3)], pass_send)
+    wait_bytes(oper.at[pl.ds(0, 7)], o_send)
 
 
 def shards(q, k, v, taps, sbias, filt, skip, weight, obias):
@@ -295,10 +297,12 @@
             pltpu.VMEM((1, 256), F32),
             pltpu.VMEM((1, 256), F32),
             pltpu.VMEM((256, LANES), F32),
+            pltpu.VMEM((512, LANES), F32),
             pltpu.VMEM((16, 256), BF16),
             pltpu.VMEM((16, 256), BF16),
             pltpu.VMEM((3, 264, 256), F32),
-            message, message, message, message, message, message,
+            pltpu.VMEM((ctx_n, 8, LANES), BF16), message, message,
+            pltpu.VMEM((ctx_n, 8, LANES), BF16), message, message,
             pltpu.VMEM((2, 2, LANES, LANES), F32),
             pltpu.VMEM((2, 2, LANES, LANES), F32),
             pltpu.VMEM((4, LANES * PHASE, LANES), BF16),
@@ -310,7 +314,7 @@
             pltpu.VMEM((ch_n, 256, 256), BF16),
             pltpu.VMEM((ch_n, 2, 256, LANES), BF16),
             pltpu.VMEM((ch_n, 2, LANES, 256), BF16),
-            dma((3, 2)), dma((3, 2)), dma((2,)), dma, dma, dma, dma((ch_n, 2)), dma, dma((9,)),
+            dma((2, 2)), dma((2, 2)), dma((2,)), dma, dma, dma, dma((ch_n, 2)), dma((9,)), dma((2,)),
         ],
         compiler_params=pltpu.CompilerParams(
             collective_id=3, has_side_effects=True, vmem_limit_bytes=63 * 2**20),

time: 59.1 us -> 57.9 us (0.980)
  Pallas kernels: 57.4 us -> 56.1 us
    pallas_call x1, Pallas kernels: 57.4 us -> 56.1 us  [shards(): pl.pallas_call(functools.partial(kernel, ctx_n, ch_n), out_shape=jax.Shap...]
where the time goes in v4:
time: 57.9 us; the launch traced here: 57.7 us
  Pallas kernels  56.1 us (97%)
  local copies, waits for them, and re-layouts  1.57 us (3%)
    pallas_call x1, Pallas kernels, shards(): pl.pallas_call(functools.partial(kernel, ctx_n, ch_n), out_shape=jax.Shap...  56.1 us
    unnamed x1, local copies, waits for them, and re-layouts  1.57 us

profile of v4, /device:TPU:1, one launch (start us, length us, event | category | flops | bytes accessed | tf_op | source)
XLA Modules:
  0.0 57.7 jit_solution(16724964052054133779)
XLA Ops:
  0.0 56.1 %shard_map.91 = bf16[256,256]{1,0:T(8,128)(2,1)} custom-call(bf16[256,256]{1,0:T(8,128)(2,1)} %q_hbm.1, bf16[256,256]{1,0:T(8,128)(2,1)} %k_hbm.1, bf16[256,256]{1,0:T(8,128)(2,1)} %v_hbm.1, f32[3,3,256]{2,1,0:T(4,128)} %taps_hbm.1, f32[3,256]{1,0:T(4,128)} %sbias_hbm.1, f32[256,256]{1,0:T(8,128)} %filt_hbm.1, f32[1,256]{1,0:T(1,128)} %bitcast.2, ...), custom_call_target="tpu_custom_call" | custom-call | tf_op jit(solution)/shard_map/pallas_call | solution.py:285
  56.2 1.6 %copy.11 = bf16[256,256]{1,0:T(8,128)(2,1)} copy(bf16[256,256]{1,0:T(8,128)(2,1)} %shard_map.91) | data formatting | bytes 262144

commit v5 on v4

--- a/solution.py
+++ b/solution.py
@@ -95,9 +95,9 @@
 
 def kernel(
     ctx_n, ch_n,
-    q_hbm, k_hbm, v_hbm, taps_hbm, sbias_hbm, filt_hbm, skip_hbm, w_ref, obias_hbm,
+    q_hbm, k_hbm, v_hbm, filt_hbm, w_ref, small_hbm,
     out_ref,
-    q_ref, k_ref, v_ref, taps_ref, sbias_ref, filt_ref, skip_ref, obias_ref,
+    q_ref, k_ref, v_ref, filt_ref, small_ref,
     flat, wide_flat, halo_out, halo_in, wide, send_h, send_g, send_y, recv_h, recv_g, recv_y,
     gated_t, query_t, toeplitz, shifted, blocks, phases, result, acc, w_all, w_t, oper,
     send_sem, recv_sem, halo_sem, w_send, w_recv, o_send, o_recv, in_sem, h_sem,
@@ -110,8 +110,7 @@
         pltpu.make_async_copy(src, dst, in_sem.at[index])
         for index, (src, dst) in enumerate((
             (filt_hbm, filt_ref), (q_hbm, q_ref), (k_hbm, k_ref), (v_hbm, v_ref),
-            (taps_hbm, taps_ref), (sbias_hbm, sbias_ref), (skip_hbm, skip_ref),
-            (obias_hbm, obias_ref),
+            (small_hbm, small_ref),
             (w_ref.at[:, pl.ds(pl.multiple_of(my_ch * 256, 256), 256)], w_all.at[my_ch])))
     ]
     fetches[0].start()
@@ -141,7 +140,7 @@
     def exchange(src, dst, which, chunk):
         @pl.loop(1, ctx_n)
         def _(step):
-            target = lax.rem(me + step, ctx_n)
+            target = lax.rem(me + 25 * step, ctx_n)
             remote(src.at[chunk, target], dst.at[chunk, me], send_sem.at[which, chunk],
                    recv_sem.at[which, chunk], "ctx", target).start()
         dst[chunk, me] = src[chunk, me]
@@ -179,7 +178,7 @@
 
     @pl.loop(1, ctx_n)
     def _(step):
-        target = lax.rem(me + step, ctx_n)
+        target = lax.rem(me + 25 * step, ctx_n)
         remote(send_h.at[target], recv_h.at[me], h_sem.at[0], h_sem.at[1], "ctx", target).start()
     recv_h[me] = send_h[me]
 
@@ -199,10 +198,10 @@
     def short(index, half, chunk):
         at, cut, slot = half * LANES, cuts[chunk], (index + 2) % 3
         return (
-            taps_ref[index, 0:1, cut] * wide[slot, pl.ds(6 + at, LANES), cut]
-            + taps_ref[index, 1:2, cut] * wide[slot, pl.ds(7 + at, LANES), cut]
-            + taps_ref[index, 2:3, cut] * wide[slot, pl.ds(8 + at, LANES), cut]
-            + sbias_ref[index:index + 1, cut]
+            small_ref[pl.ds(3 * index + 0, 1), cut] * wide[slot, pl.ds(6 + at, LANES), cut]
+            + small_ref[pl.ds(3 * index + 1, 1), cut] * wide[slot, pl.ds(7 + at, LANES), cut]
+            + small_ref[pl.ds(3 * index + 2, 1), cut] * wide[slot, pl.ds(8 + at, LANES), cut]
+            + small_ref[pl.ds(9 + index, 1), cut]
         )
 
     for chunk in range(2):
@@ -243,7 +242,7 @@
                       o_recv.at[source, chunk], "ch", target)
 
     for chunk in range(2):
-        skip_t = jnp.broadcast_to(skip_ref[:, cuts[chunk]], (LANES, LANES)).T
+        skip_t = jnp.broadcast_to(small_ref[12:13, cuts[chunk]], (LANES, LANES)).T
         arrived(recv_y, 1, chunk)
         unpack(chunk, recv_y)
         for half in range(2):
@@ -254,7 +253,7 @@
         for hop in (4, 3, 5, 2, 6, 1, 7):
             pass_on(my_ch, chunk, o_send, lax.rem(my_ch + hop, ch_n)).start()
 
-    bias_t = jnp.broadcast_to(obias_ref[...], (LANES, 256)).T
+    bias_t = jnp.broadcast_to(small_ref[13:14, :], (LANES, 256)).T
     total = jnp.concatenate([bias_t, bias_t], axis=1)
 
     def add(total, source, chunk):
@@ -282,20 +281,19 @@
     vmem = pl.BlockSpec(memory_space=pltpu.VMEM)
     message = pltpu.VMEM((2, ctx_n, 4, LANES), BF16)
     dma = pltpu.SemaphoreType.DMA
+    small = jnp.concatenate(
+        [taps.reshape(9, -1), sbias, skip.reshape(1, -1), obias.reshape(1, -1)], axis=0)
     return pl.pallas_call(
         functools.partial(kernel, ctx_n, ch_n),
         out_shape=jax.ShapeDtypeStruct((256, 256), BF16),
-        in_specs=[pl.BlockSpec(memory_space=pl.ANY)] * 9,
+        in_specs=[pl.BlockSpec(memory_space=pl.ANY)] * 6,
         out_specs=vmem,
         scratch_shapes=[
             pltpu.VMEM((256, 256), BF16),
             pltpu.VMEM((256, 256), BF16),
             pltpu.VMEM((256, 256), BF16),
-            pltpu.VMEM((3, 3, 256), F32),
-            pltpu.VMEM((3, 256), F32),
             pltpu.VMEM((256, 256), F32),
-            pltpu.VMEM((1, 256), F32),
-            pltpu.VMEM((1, 256), F32),
+            pltpu.VMEM((14, 256), F32),
             pltpu.VMEM((256, LANES), F32),
             pltpu.VMEM((512, LANES), F32),
             pltpu.VMEM((16, 256), BF16),
@@ -314,11 +312,11 @@
             pltpu.VMEM((ch_n, 256, 256), BF16),
             pltpu.VMEM((ch_n, 2, 256, LANES), BF16),
             pltpu.VMEM((ch_n, 2, LANES, 256), BF16),
-            dma((2, 2)), dma((2, 2)), dma((2,)), dma, dma, dma, dma((ch_n, 2)), dma((9,)), dma((2,)),
+            dma((2, 2)), dma((2, 2)), dma((2,)), dma, dma, dma, dma((ch_n, 2)), dma((6,)), dma((2,)),
         ],
         compiler_params=pltpu.CompilerParams(
-            collective_id=3, has_side_effects=True, vmem_limit_bytes=63 * 2**20),
-    )(q, k, v, taps, sbias, filt, skip.reshape(1, -1), weight, obias.reshape(1, -1))
+            collective_id=3, has_side_effects=True, vmem_limit_bytes=54 * 2**20 - 256 * 1024),
+    )(q, k, v, filt, weight, small)
 
 
 def solution(mesh):

time: 57.9 us -> 57.1 us (0.986)
  Pallas kernels: 56.1 us -> 55.5 us
    unnamed x1 -> x7, local copies, waits for them, and re-layouts: 1.57 us -> 0.67 us
    reshape x0 -> x1, local copies, waits for them, and re-layouts: none -> 0.75 us  [shards(): taps.reshape(9, -1)]
    pallas_call x1, Pallas kernels: 56.1 us -> 55.5 us  [shards(): pl.pallas_call(functools.partial(kernel, ctx_n, ch_n), out_shape=jax.Shap...]
where the time goes in v5:
time: 57.1 us; the launch traced here: 56.9 us
  Pallas kernels  55.5 us (97%)
  local copies, waits for them, and re-layouts  1.42 us (2%)
    pallas_call x1, Pallas kernels, shards(): pl.pallas_call(functools.partial(kernel, ctx_n, ch_n), out_shape=jax.Shap...  55.5 us

profile of v5, /device:TPU:1, one launch (start us, length us, event | category | flops | bytes accessed | tf_op | source)
XLA Modules:
  0.0 56.9 jit_solution(3952227528126691654)
XLA Ops:
  0.0 0.0 copy-start
  0.0 0.0 copy-start.1
  0.0 0.0 copy-start.2
  0.0 0.8 %reshape.9 = f32[9,256]{1,0:T(8,128)S(1)} reshape(f32[3,3,256]{2,1,0:T(4,128)} %param.12) | data formatting | bytes 18432 | tf_op jit(solution)/shard_map/reshape | solution.py:285
  0.8 0.0 copy-done
  0.8 0.0 copy-done.1
  0.8 0.0 copy-done.2
  0.8 55.5 %shard_map.91 = bf16[256,256]{1,0:T(8,128)(2,1)S(1)} custom-call(bf16[256,256]{1,0:T(8,128)(2,1)} %q_hbm.1, bf16[256,256]{1,0:T(8,128)(2,1)} %k_hbm.1, bf16[256,256]{1,0:T(8,128)(2,1)} %v_hbm.1, f32[256,256]{1,0:T(8,128)} %filt_hbm.1, bf16[256,2048]{1,0:T(8,128)(2,1)} %w_ref.1, f32[14,256]{1,0:T(8,128)S(1)} %pad_maximum_fusion.small_hbm), custom_call_target="tpu_custom_call" | custom-call | tf_op jit(solution)/shard_map/pallas_call | solution.py:286
  56.3 0.7 %copy.11 = bf16[256,256]{1,0:T(8,128)(2,1)} copy(bf16[256,256]{1,0:T(8,128)(2,1)S(1)} %shard_map.91) | data formatting | bytes 262144
  (1 shorter events, 0.0 us)
Async XLA Ops:
  0.0 0.8 %copy-start = (f32[3,256]{1,0:T(4,128)S(1)}, f32[3,256]{1,0:T(4,128)}, u32[]{:S(2)}) copy-start(f32[3,256]{1,0:T(4,128)} %param.13) | copy-start | bytes 9220
  0.0 0.8 %copy-start.1 = (f32[256]{0:T(256)S(1)}, f32[256]{0:T(256)}, u32[]{:S(2)}) copy-start(f32[256]{0:T(256)} %param.17) | copy-start | bytes 3076
  0.0 0.8 %copy-start.2 = (f32[256]{0:T(256)S(1)}, f32[256]{0:T(256)}, u32[]{:S(2)}) copy-start(f32[256]{0:T(256)} %param.15) | copy-start | bytes 3076

commit v6 on v5

--- a/solution.py
+++ b/solution.py
@@ -198,10 +198,10 @@
     def short(index, half, chunk):
         at, cut, slot = half * LANES, cuts[chunk], (index + 2) % 3
         return (
-            small_ref[pl.ds(3 * index + 0, 1), cut] * wide[slot, pl.ds(6 + at, LANES), cut]
-            + small_ref[pl.ds(3 * index + 1, 1), cut] * wide[slot, pl.ds(7 + at, LANES), cut]
-            + small_ref[pl.ds(3 * index + 2, 1), cut] * wide[slot, pl.ds(8 + at, LANES), cut]
-            + small_ref[pl.ds(9 + index, 1), cut]
+            small_ref[index, 0:1, cut] * wide[slot, pl.ds(6 + at, LANES), cut]
+            + small_ref[index, 1:2, cut] * wide[slot, pl.ds(7 + at, LANES), cut]
+            + small_ref[index, 2:3, cut] * wide[slot, pl.ds(8 + at, LANES), cut]
+            + small_ref[3, index:index + 1, cut]
         )
 
     for chunk in range(2):
@@ -242,7 +242,7 @@
                       o_recv.at[source, chunk], "ch", target)
 
     for chunk in range(2):
-        skip_t = jnp.broadcast_to(small_ref[12:13, cuts[chunk]], (LANES, LANES)).T
+        skip_t = jnp.broadcast_to(small_ref[4, 0:1, cuts[chunk]], (LANES, LANES)).T
         arrived(recv_y, 1, chunk)
         unpack(chunk, recv_y)
         for half in range(2):
@@ -253,7 +253,7 @@
         for hop in (4, 3, 5, 2, 6, 1, 7):
             pass_on(my_ch, chunk, o_send, lax.rem(my_ch + hop, ch_n)).start()
 
-    bias_t = jnp.broadcast_to(small_ref[13:14, :], (LANES, 256)).T
+    bias_t = jnp.broadcast_to(small_ref[4, 1:2, :], (LANES, 256)).T
     total = jnp.concatenate([bias_t, bias_t], axis=1)
 
     def add(total, source, chunk):
@@ -282,7 +282,7 @@
     message = pltpu.VMEM((2, ctx_n, 4, LANES), BF16)
     dma = pltpu.SemaphoreType.DMA
     small = jnp.concatenate(
-        [taps.reshape(9, -1), sbias, skip.reshape(1, -1), obias.reshape(1, -1)], axis=0)
+        [taps, sbias[None], jnp.stack([skip, obias, obias])[None]], axis=0)
     return pl.pallas_call(
         functools.partial(kernel, ctx_n, ch_n),
         out_shape=jax.ShapeDtypeStruct((256, 256), BF16),
@@ -293,7 +293,7 @@
             pltpu.VMEM((256, 256), BF16),
             pltpu.VMEM((256, 256), BF16),
             pltpu.VMEM((256, 256), F32),
-            pltpu.VMEM((14, 256), F32),
+            pltpu.VMEM((5, 3, 256), F32),
             pltpu.VMEM((256, LANES), F32),
             pltpu.VMEM((512, LANES), F32),
             pltpu.VMEM((16, 256), BF16),

time: 57.1 us -> 57.8 us (1.012)
  other arithmetic: 0.01 us -> 0.72 us
    reshape x1 -> x0, local copies, waits for them, and re-layouts: 0.75 us -> none  [shards(): taps.reshape(9, -1)]
    concatenate x1, other arithmetic: 0.01 us -> 0.71 us  [shards(): jnp.concatenate([taps, sbias[None], jnp.stack([skip, obias, obias])[None]...]
    unnamed x7, local copies, waits for them, and re-layouts: 0.67 us -> 1.36 us
where the time goes in v6:
time: 57.8 us; the launch traced here: 57.5 us
  Pallas kernels  55.4 us (96%)
  local copies, waits for them, and re-layouts  1.36 us (2%)
  other arithmetic  0.72 us (1%)
    pallas_call x1, Pallas kernels, shards(): pl.pallas_call(functools.partial(kernel, ctx_n, ch_n), out_shape=jax.Shap...  55.4 us
    unnamed x7, local copies, waits for them, and re-layouts  1.36 us

profile of v6, /device:TPU:1, one launch (start us, length us, event | category | flops | bytes accessed | tf_op | source)
XLA Modules:
  0.0 57.5 jit_solution(13152441356437045279)
XLA Ops:
  0.0 0.0 copy-start.1
  0.0 0.0 copy-start.2
  0.0 0.0 copy-start
  0.0 0.7 %copy-done.1 = f32[256]{0:T(256)S(1)} copy-done((f32[256]{0:T(256)S(1)}, f32[256]{0:T(256)}, u32[]{:S(2)}) %copy-start.1) | copy-done | bytes 1048
  0.7 0.0 copy-done.2
  0.7 0.0 copy-done
  0.7 0.7 %pad_maximum_fusion.small_hbm = f32[5,3,256]{2,1,0:T(4,128)S(1)} fusion(f32[1,3,256]{2,1,0:T(4,128)S(1)} %maximum_bitcast_fusion, f32[1,3,256]{2,1,0:T(4,128)S(1)} %bitcast.5, f32[3,3,256]{2,1,0:T(4,128)} %param.12), kind=kLoop, calls=%fused_computation | loop fusion | flops 7680 | bytes 30720 | tf_op jit(solution)/shard_map/concatenate | solution.py:284
  1.4 55.4 %shard_map.91 = bf16[256,256]{1,0:T(8,128)(2,1)S(1)} custom-call(bf16[256,256]{1,0:T(8,128)(2,1)} %q_hbm.1, bf16[256,256]{1,0:T(8,128)(2,1)} %k_hbm.1, bf16[256,256]{1,0:T(8,128)(2,1)} %v_hbm.1, f32[256,256]{1,0:T(8,128)} %filt_hbm.1, bf16[256,2048]{1,0:T(8,128)(2,1)} %w_ref.1, f32[5,3,256]{2,1,0:T(4,128)S(1)} %pad_maximum_fusion.small_hbm), custom_call_target="tpu_custom_call" | custom-call | tf_op jit(solution)/shard_map/pallas_call | solution.py:286
  56.9 0.7 %copy.11 = bf16[256,256]{1,0:T(8,128)(2,1)} copy(bf16[256,256]{1,0:T(8,128)(2,1)S(1)} %shard_map.91) | data formatting | bytes 262144
  (1 shorter events, 0.0 us)
Async XLA Ops:
  0.0 0.7 %copy-start.1 = (f32[256]{0:T(256)S(1)}, f32[256]{0:T(256)}, u32[]{:S(2)}) copy-start(f32[256]{0:T(256)} %param.17) | copy-start | bytes 3076
  0.0 0.7 %copy-start.2 = (f32[256]{0:T(256)S(1)}, f32[256]{0:T(256)}, u32[]{:S(2)}) copy-start(f32[256]{0:T(256)} %param.15) | copy-start | bytes 3076
  0.0 0.7 %copy-start = (f32[3,256]{1,0:T(4,128)S(1)}, f32[3,256]{1,0:T(4,128)}, u32[]{:S(2)}) copy-start(f32[3,256]{1,0:T(4,128)} %param.13) | copy-start | bytes 9220
